TPU v7x, 256 devices: a whole 4x4x8 slice. The times are simulated.
256 devices in a mesh: row: 16 (over z, x_lo), col: 16 (over x_hi, y, core).
Axes of the slice: x: 4 (x_hi: 2, x_lo: 2; x = x_hi * 2 + x_lo), y: 4, z: 8, core: 2. Of those that a mesh axis runs over, the one named last changes fastest.
Arguments:
- src_points: bfloat16 [64, 16384], P(None, ('row', 'col')), may hold values from -24 to 24
- tgt_points: bfloat16 [64, 16384], P(None, ('col', 'row')), may hold values from -24 to 24
- grad_f: float32 [16384], P('row'), may hold values from -6 to 6
- grad_g: float32 [16384], P('col'), may hold values from -6 to 6
Outputs:
- grad_src: float32 [64, 16384], P(None, ('row', 'col'))
- grad_tgt: float32 [64, 16384], P(None, ('col', 'row'))
All inputs are finite; a program needn't handle non-finite values.
Results may differ from a plain program's by a relative error of at most 0.0085.
Values may be sent and summed in bfloat16 or wider, within the bound.
A program may use at most 64 MiB of HBM per device.

v0:
```python
import math

import jax
import jax.numpy as jnp
from jax import lax
from jax.sharding import PartitionSpec as P

SINK = 2
CG = 3


EPS = 4.0
TAU = 0.1


def cost_tile(block_pts, block_sq, points_col, sq_col):
    cross = lax.dot_general(
        block_pts, points_col, (((0,), (0,)), ((), ())), preferred_element_type=jnp.float32
    )
    return block_sq[:, None] + sq_col[None, :] - 2.0 * cross


def body(src_points, tgt_points, grad_f, grad_g):
    points_row = lax.all_gather(src_points, "col", axis=1, tiled=True)
    points_col = lax.all_gather(tgt_points, "row", axis=1, tiled=True)
    sq_row = jnp.sum(jnp.square(points_row.astype(jnp.float32)), axis=0)
    sq_col = jnp.sum(jnp.square(points_col.astype(jnp.float32)), axis=0)
    features, row_count = points_row.shape
    col_count = points_col.shape[1]
    block = min(512, row_count)
    block_count = row_count // block
    blocks_pts = jnp.moveaxis(points_row.reshape(features, block_count, block), 1, 0)
    blocks_sq = sq_row.reshape(block_count, block)
    shift = EPS * math.log(lax.axis_size("row") / lax.axis_size("col"))
    pot_col = jnp.zeros((col_count,), jnp.float32)
    pot_row = jnp.zeros((row_count,), jnp.float32)
    for iteration in range(SINK):

        def row_scores(block_pts, block_sq):
            return (pot_col[None, :] - cost_tile(block_pts, block_sq, points_col, sq_col)) / EPS

        def maxima(pieces):
            return jnp.max(row_scores(pieces[0], pieces[1]), axis=1)

        row_highest = lax.pmax(lax.map(maxima, (blocks_pts, blocks_sq)).reshape(-1), "col")

        def sums(pieces):
            return jnp.sum(jnp.exp(row_scores(pieces[0], pieces[1]) - pieces[2][:, None]), axis=1)

        local = lax.map(
            sums, (blocks_pts, blocks_sq, row_highest.reshape(block_count, block))
        ).reshape(-1)
        row_totals = lax.psum(local, "col")
        pot_row = -EPS * (row_highest + jnp.log(row_totals))
        blocks_pot = pot_row.reshape(block_count, block)

        def scores(pieces):
            return (pieces[2][:, None] - cost_tile(pieces[0], pieces[1], points_col, sq_col)) / EPS

        lowest = jnp.full((col_count,), -jnp.inf, jnp.float32)
        empty = jnp.zeros((col_count,), jnp.float32)

        def max_step(carry, pieces):
            return (jnp.maximum(carry, jnp.max(scores(pieces), axis=0)), None)

        highest, unused = lax.scan(max_step, lowest, (blocks_pts, blocks_sq, blocks_pot))
        highest = lax.pmax(highest, "row")

        def sum_step(carry, pieces):
            return (carry + jnp.sum(jnp.exp(scores(pieces) - highest[None, :]), axis=0), None)

        totals, unused = lax.scan(sum_step, empty, (blocks_pts, blocks_sq, blocks_pot))
        totals = lax.psum(totals, "row")
        pot_col = shift - EPS * (highest + jnp.log(totals))

    def plan_rows(pieces):
        cost = cost_tile(pieces[0], pieces[1], points_col, sq_col)
        return jnp.exp((pieces[2][:, None] + pot_col[None, :] - cost) / EPS).astype(jnp.bfloat16)

    plan_tile = lax.map(
        plan_rows, (blocks_pts, blocks_sq, pot_row.reshape(block_count, block))
    ).reshape(row_count, col_count)

    def row_dot(vector):
        return jnp.sum(plan_tile * vector[None, :], axis=1)

    def col_dot(vector):
        return jnp.sum(plan_tile * vector[:, None], axis=0)

    row_mass = lax.psum(jnp.sum(plan_tile, axis=1, dtype=jnp.float32), "col")
    col_mass, pulled = lax.psum(
        (jnp.sum(plan_tile, axis=0, dtype=jnp.float32), col_dot(grad_f / row_mass)), "row"
    )
    rhs = grad_g - pulled

    def norm_sum(vector):
        return lax.psum(jnp.sum(vector * vector), "col")

    dual_col = jnp.zeros_like(rhs)
    residual = rhs
    direction = rhs
    norm_now = norm_sum(residual)
    for iteration in range(CG):
        applied = lax.psum(row_dot(direction), "col")
        back = lax.psum(col_dot(applied / row_mass), "row")
        image = (1.0 + TAU) * col_mass * direction - back
        alpha = norm_now / lax.psum(jnp.sum(direction * image), "col")
        dual_col = dual_col + alpha * direction
        residual = residual - alpha * image
        norm_next = norm_sum(residual)
        direction = residual + norm_next / norm_now * direction
        norm_now = norm_next
    dual_row = (grad_f - lax.psum(row_dot(dual_col), "col")) / row_mass
    weights = (plan_tile * (dual_row[:, None] + dual_col[None, :])).astype(jnp.bfloat16)
    rows_w = jnp.sum(weights, axis=1, dtype=jnp.float32)
    cols_w = jnp.sum(weights, axis=0, dtype=jnp.float32)
    pulled_src = lax.dot_general(
        points_col, weights, (((1,), (1,)), ((), ())), preferred_element_type=jnp.float32
    )
    pulled_tgt = lax.dot_general(
        points_row, weights, (((1,), (0,)), ((), ())), preferred_element_type=jnp.float32
    )
    part_src = 2.0 * (points_row.astype(jnp.float32) * rows_w[None, :] - pulled_src)
    part_tgt = 2.0 * (points_col.astype(jnp.float32) * cols_w[None, :] - pulled_tgt)
    total_src = lax.psum(part_src, "col")
    total_tgt = lax.psum(part_tgt, "row")
    width_src = row_count // lax.axis_size("col")
    width_tgt = col_count // lax.axis_size("row")
    grad_src = lax.dynamic_slice_in_dim(total_src, lax.axis_index("col") * width_src, width_src, 1)
    grad_tgt = lax.dynamic_slice_in_dim(total_tgt, lax.axis_index("row") * width_tgt, width_tgt, 1)
    return (grad_src, grad_tgt)


def solution(mesh):
    in_specs = (P(None, ("row", "col")), P(None, ("col", "row")), P("row"), P("col"))
    out_specs = (P(None, ("row", "col")), P(None, ("col", "row")))
    return jax.shard_map(body, mesh=mesh, in_specs=in_specs, out_specs=out_specs, check_vma=False)
```

profile of v0, /device:TPU:1, one launch (start us, length us, event | category | flops | bytes accessed | tf_op | source)
XLA Modules:
  0.0 1109.5 jit_solution(16493199737781712499)
XLA Ops:
  8.1 31.7 %all_gather.7 = bf16[64,1024]{0,1:T(8,128)(2,1)S(1)} all-gather(bf16[64,64]{0,1:T(8,128)(2,1)S(1)} %copy.9), channel_id=1, replica_groups=mesh['row'=16,'col'=16] {'row'}, dimensions={1}, use_global_device_ids=true | all-gather | bytes 139264 | tf_op jit(solution)/shard_map/all_gather | solution.py:25
  40.7 32.1 %all_gather.6 = bf16[64,1024]{0,1:T(8,128)(2,1)S(1)} all-gather(bf16[64,64]{0,1:T(8,128)(2,1)S(1)} %copy.7), channel_id=1, replica_groups=mesh['row'=16,'col'=16] {'col'}, dimensions={1}, use_global_device_ids=true | all-gather | bytes 139264 | tf_op jit(solution)/shard_map/all_gather | solution.py:24
  73.2 1.5 while.94
  74.8 32.7 %pmax.28 = f32[1024]{0:T(1024)S(1)} all-reduce(f32[1024]{0:T(1024)S(1)} %bitcast.213), channel_id=1, replica_groups=mesh['row'=16,'col'=16] {'col'}, use_global_device_ids=true, to_apply=%region_5.6 | all-reduce | flops 1024 | bytes 8192 | tf_op jit(solution)/shard_map/pmax | solution.py:45
  107.4 1.9 while.95
  107.5 0.9 exponential_reduce_fusion.8
  108.4 0.9 exponential_reduce_fusion.8
  109.4 33.5 %psum.154 = f32[1024]{0:T(1024)S(1)} all-reduce(f32[1024]{0:T(1024)S(1)} %bitcast.214), channel_id=1, replica_groups=mesh['row'=16,'col'=16] {'col'}, use_global_device_ids=true, to_apply=%region_9.10 | all-reduce | flops 1024 | bytes 8192 | tf_op jit(solution)/shard_map/psum | solution.py:53
  142.9 1.3 while.99
  144.3 23.7 %pmax.29 = f32[1024]{0:T(1024)S(1)} all-reduce(f32[1024]{0:T(1024)S(1)} %get-tuple-element.352), channel_id=1, replica_groups=mesh['row'=16,'col'=16] {'row'}, use_global_device_ids=true, to_apply=%region_13.14 | all-reduce | flops 1024 | bytes 8192 | tf_op jit(solution)/shard_map/pmax | solution.py:67
  167.9 1.8 while.100
  168.0 0.8 exponential_reduce_fusion.10
  169.7 25.5 %psum.155 = f32[1024]{0:T(1024)S(1)} all-reduce(f32[1024]{0:T(1024)S(1)} %get-tuple-element.353), channel_id=1, replica_groups=mesh['row'=16,'col'=16] {'row'}, use_global_device_ids=true, to_apply=%region_17.18 | all-reduce | flops 1024 | bytes 8192 | tf_op jit(solution)/shard_map/psum | solution.py:73
  195.2 1.5 while.96
  196.7 47.3 %pmax.30 = f32[1024]{0:T(1024)S(1)} all-reduce(f32[1024]{0:T(1024)S(1)} %bitcast.215), channel_id=1, replica_groups=mesh['row'=16,'col'=16] {'col'}, use_global_device_ids=true, to_apply=%region_21.22 | all-reduce | flops 1024 | bytes 8192 | tf_op jit(solution)/shard_map/pmax | solution.py:45
  244.0 1.9 while.97
  244.1 0.9 exponential_reduce_fusion.9
  245.0 0.9 exponential_reduce_fusion.9
  246.0 33.2 %psum.156 = f32[1024]{0:T(1024)S(1)} all-reduce(f32[1024]{0:T(1024)S(1)} %bitcast.216), channel_id=1, replica_groups=mesh['row'=16,'col'=16] {'col'}, use_global_device_ids=true, to_apply=%region_25.26 | all-reduce | flops 1024 | bytes 8192 | tf_op jit(solution)/shard_map/psum | solution.py:53
  279.2 1.3 while.101
  280.5 23.7 %pmax.31 = f32[1024]{0:T(1024)S(1)} all-reduce(f32[1024]{0:T(1024)S(1)} %get-tuple-element.356), channel_id=1, replica_groups=mesh['row'=16,'col'=16] {'row'}, use_global_device_ids=true, to_apply=%region_29.30 | all-reduce | flops 1024 | bytes 8192 | tf_op jit(solution)/shard_map/pmax | solution.py:67
  304.2 1.8 while.102
  304.2 0.8 exponential_reduce_fusion.11
  305.1 0.8 exponential_reduce_fusion.11
  305.9 25.5 %psum.157 = f32[1024]{0:T(1024)S(1)} all-reduce(f32[1024]{0:T(1024)S(1)} %get-tuple-element.357), channel_id=1, replica_groups=mesh['row'=16,'col'=16] {'row'}, use_global_device_ids=true, to_apply=%region_33.34 | all-reduce | flops 1024 | bytes 8192 | tf_op jit(solution)/shard_map/psum | solution.py:73
  331.4 1.7 while.98
  333.1 0.9 convert_reduce_fusion
  334.0 47.3 %psum.158 = f32[1024]{0:T(1024)S(1)} all-reduce(f32[1024]{0:T(1024)S(1)} %bitcast.217), channel_id=1, replica_groups=mesh['row'=16,'col'=16] {'col'}, use_global_device_ids=true, to_apply=%region_37.38 | all-reduce | flops 1024 | bytes 8192 | tf_op jit(solution)/shard_map/psum | solution.py:90
  381.8 23.7 %psum.159 = f32[1024]{0:T(1024)S(1)} all-reduce(f32[1024]{0:T(1024)S(1)} %fusion.29), channel_id=1, replica_groups=mesh['row'=16,'col'=16] {'row'}, use_global_device_ids=true, to_apply=%region_39.40 | all-reduce | flops 1024 | bytes 8192 | tf_op jit(solution)/shard_map/psum | solution.py:91
  406.0 40.1 %psum.162 = f32[1024]{0:T(1024)S(1)} all-reduce(f32[1024]{0:T(1024)S(1)} %bitcast.218), channel_id=1, replica_groups=mesh['row'=16,'col'=16] {'col'}, use_global_device_ids=true, to_apply=%region_45.46 | all-reduce | flops 1024 | bytes 8192 | tf_op jit(solution)/shard_map/psum | solution.py:104
  446.6 26.2 %all-reduce.1 = (f32[1024]{0:T(1024)S(1)}, f32[1024]{0:T(1024)S(1)}) all-reduce(f32[1024]{0:T(1024)S(1)} %fusion.31, f32[1024]{0:T(1024)S(1)} %get-tuple-element.529), channel_id=1, replica_groups=mesh['row'=16,'col'=16] {'row'}, use_global_device_ids=true, to_apply=%region_47.48 | all-reduce | flops 2048 | bytes 16384 | tf_op jit(solution)/shard_map/psum | solution.py:105
  473.4 40.8 %all-reduce = (f32[]{:T(128)}, f32[]{:T(128)}) all-reduce(f32[]{:T(128)} %get-tuple-element.532, f32[]{:T(128)} %get-tuple-element.531), channel_id=1, replica_groups=mesh['row'=16,'col'=16] {'col'}, use_global_device_ids=true, to_apply=%region_41.42 | all-reduce | flops 2 | bytes 16 | tf_op jit(solution)/shard_map/psum | solution.py:97
  516.2 34.0 %psum.165 = f32[]{:T(128)} all-reduce(f32[]{:T(128)} %get-tuple-element.671), channel_id=1, replica_groups=mesh['row'=16,'col'=16] {'col'}, use_global_device_ids=true, to_apply=%region_51.52 | all-reduce | flops 1 | bytes 8 | tf_op jit(solution)/shard_map/psum | solution.py:97
  551.9 33.2 %psum.166 = f32[1024]{0:T(1024)S(1)} all-reduce(f32[1024]{0:T(1024)S(1)} %bitcast.219), channel_id=1, replica_groups=mesh['row'=16,'col'=16] {'col'}, use_global_device_ids=true, to_apply=%region_53.54 | all-reduce | flops 1024 | bytes 8192 | tf_op jit(solution)/shard_map/psum | solution.py:104
  585.6 23.7 %psum.167 = f32[1024]{0:T(1024)S(1)} all-reduce(f32[1024]{0:T(1024)S(1)} %fusion.33), channel_id=1, replica_groups=mesh['row'=16,'col'=16] {'row'}, use_global_device_ids=true, to_apply=%region_55.56 | all-reduce | flops 1024 | bytes 8192 | tf_op jit(solution)/shard_map/psum | solution.py:105
  609.9 40.7 %psum.168 = f32[]{:T(128)} all-reduce(f32[]{:T(128)} %multiply_reduce_fusion.6), channel_id=1, replica_groups=mesh['row'=16,'col'=16] {'col'}, use_global_device_ids=true, to_apply=%region_57.58 | all-reduce | flops 1 | bytes 8 | tf_op jit(solution)/shard_map/psum | solution.py:107
  652.6 33.8 %psum.169 = f32[]{:T(128)} all-reduce(f32[]{:T(128)} %get-tuple-element.669), channel_id=1, replica_groups=mesh['row'=16,'col'=16] {'col'}, use_global_device_ids=true, to_apply=%region_59.60 | all-reduce | flops 1 | bytes 8 | tf_op jit(solution)/shard_map/psum | solution.py:97
  688.2 33.2 %psum.170 = f32[1024]{0:T(1024)S(1)} all-reduce(f32[1024]{0:T(1024)S(1)} %bitcast.220), channel_id=1, replica_groups=mesh['row'=16,'col'=16] {'col'}, use_global_device_ids=true, to_apply=%region_61.62 | all-reduce | flops 1024 | bytes 8192 | tf_op jit(solution)/shard_map/psum | solution.py:104
  721.9 25.6 %psum.171 = f32[1024]{0:T(1024)S(1)} all-reduce(f32[1024]{0:T(1024)S(1)} %fusion.35), channel_id=1, replica_groups=mesh['row'=16,'col'=16] {'row'}, use_global_device_ids=true, to_apply=%region_63.64 | all-reduce | flops 1024 | bytes 8192 | tf_op jit(solution)/shard_map/psum | solution.py:105
  748.1 40.8 %psum.172 = f32[]{:T(128)} all-reduce(f32[]{:T(128)} %multiply_reduce_fusion.4), channel_id=1, replica_groups=mesh['row'=16,'col'=16] {'col'}, use_global_device_ids=true, to_apply=%region_65.66 | all-reduce | flops 1 | bytes 8 | tf_op jit(solution)/shard_map/psum | solution.py:107
  790.7 33.2 %psum.173 = f32[1024]{0:T(1024)S(1)} all-reduce(f32[1024]{0:T(1024)S(1)} %bitcast.221), channel_id=1, replica_groups=mesh['row'=16,'col'=16] {'col'}, use_global_device_ids=true, to_apply=%region_67.68 | all-reduce | flops 1024 | bytes 8192 | tf_op jit(solution)/shard_map/psum | solution.py:113
  824.5 1.0 convert_reduce_fusion.2
  825.8 1.2 fusion.40
  827.2 3.1 fusion.42
  830.3 115.7 %all-reduce.7.cloned.1.call-done = f32[64,1024]{1,0:T(8,128)} async-done(((f32[64,1024]{1,0:T(8,128)}), f32[64,1024]{1,0:T(8,128)}) %all-reduce.7.cloned.1.call-update) | async-done | bytes 262160 | tf_op jit(solution)/shard_map/psum | solution.py:126
  946.0 1.4 constant_dynamic-slice_fusion.16
  947.5 153.7 %all-reduce.5.cloned.1.call-done = f32[64,1024]{1,0:T(8,128)} async-done(((f32[64,1024]{1,0:T(8,128)}), f32[64,1024]{1,0:T(8,128)}) %all-reduce.5.cloned.1.call-update) | async-done | bytes 262160 | tf_op jit(solution)/shard_map/psum | solution.py:125
  1101.2 1.4 constant_dynamic-slice_fusion.17
  (118 shorter events, 18.5 us)
Async XLA Ops:
  7.2 938.8 %all-reduce.7.cloned.1.call-start = ((), (), s32[]{:S(2)}) async-start(), calls=%async_computation.1 | async-start | bytes 524288 | tf_op jit(solution)/shard_map/psum | solution.py:126
  333.1 48.2 %copy-start.1 = (f32[1024]{0:T(1024)S(1)}, f32[1024]{0:T(1024)}, u32[]{:S(2)}) copy-start(f32[1024]{0:T(1024)} %param.24) | copy-start | bytes 12292
  333.1 72.4 %copy-start.2 = (f32[1024]{0:T(1024)S(1)}, f32[1024]{0:T(1024)}, u32[]{:S(2)}) copy-start(f32[1024]{0:T(1024)} %param.25) | copy-start | bytes 12292
  824.5 1.4 copy-start
  827.1 274.1 %all-reduce.5.cloned.1.call-start = ((), (), s32[]{:S(2)}) async-start(), calls=%async_computation | async-start | bytes 524288 | tf_op jit(solution)/shard_map/psum | solution.py:125
Sparse Core Ops, SparseCore 0:
  827.2 118.7 all-reduce.6
  948.8 152.3 all-reduce.4
where the time goes:
time: 1110 us
  blocking collectives  785 us (71%)
  waiting for transfers between devices  270 us (24%)
  between operations  21.1 us (2%)
  matrix products  18 us (2%)
    psum x1, waiting for transfers between devices, body(): total_src = lax.psum(part_src, 'col')  154 us
    psum x1, waiting for transfers between devices, body(): total_tgt = lax.psum(part_tgt, 'row')  116 us
    psum x3, blocking collectives, norm_sum(): return lax.psum(jnp.sum(vector * vector), 'col')  108 us
    psum x3, blocking collectives, body(): applied = lax.psum(row_dot(direction), 'col')  106 us
    psum x2, blocking collectives, body(): alpha = norm_now / lax.psum(jnp.sum(direction * image), 'col')  81.5 us
    pmax x2, blocking collectives, body(): lax.pmax(lax.map(maxima, (blocks_pts, blocks_sq)).reshape(-1), 'col')  80 us
    psum x3, blocking collectives, body(): back = lax.psum(col_dot(applied / row_mass), 'row')  75.5 us
    psum x2, blocking collectives, body(): row_totals = lax.psum(local, 'col')  66.7 us
  transfers between devices with their start and end apart: 2, of which 2 were waited for; matrix products, arithmetic and copies ran while one was open for 0% of the time, Pallas kernels for 0%

commit v1 on v0

v1 whole, which is shorter than its diff:
```python
import functools

import jax
import jax.numpy as jnp
from jax import lax
from jax.experimental import pallas as pl
from jax.experimental.pallas import tpu as pltpu
from jax.sharding import PartitionSpec as P

CG = 3
TAU = 0.1
LANES = 128
MESH = pl.DeviceIdType.MESH
F32 = jnp.float32
BF16 = jnp.bfloat16

LR1, LC1, LR2, LC2, MASS, PULL, CMASS, A1 = range(8)
ROUNDS = 12


def ring(d, n):
    return min(d % n, n - d % n)


def kernel(
    sizes, src_ref, tgt_ref, gf_ref, gg_ref, osrc_ref, otgt_ref,
    pack_a, pack_b, gath_a, gath_b, gown_a, gown_b, gsl_a, gsl_b,
    x_ref, y_ref, c_ref, p_ref, fe_ref, lhs_ref, row_ref, acc_ref,
    mine, slots, emine, eslots, part_a, part_b, rs_a, rs_b,
    gsem, ssem, rsem, essem, ersem,
):
    nx, ny, nz, nc = sizes
    na, nb = nx * ny, nz * nc
    row, col = lax.axis_index("row"), lax.axis_index("col")
    z, x_lo = row // 2, row % 2
    x_hi, y, core = col // (2 * ny), (col // 2) % ny, col % 2
    x = x_hi * 2 + x_lo
    me_a, me_b = x * ny + y, z * nc + core
    feats, pts = src_ref.shape
    half = feats // 2
    ti, tj = na * pts, nb * pts
    ki, kj = ti // LANES, tj // LANES

    offs_a = [(i, j) for i in range(nx) for j in range(ny) if i or j]
    offs_a.sort(key=lambda o: -(ring(o[0], nx) + ring(o[1], ny)))
    offs_b = [(i, j) for i in range(nz) for j in range(nc) if i or j]
    offs_b.sort(key=lambda o: -(ring(o[0], nz) + 0.1 * o[1]))
    peers_a, peers_b = [], []
    for dx, dy in offs_a:
        px, py = (x + dx) % nx, (y + dy) % ny
        peers_a.append(((z * 2 + px % 2, (px // 2) * (2 * ny) + py * 2 + core), px * ny + py))
    for dz, dc in offs_b:
        pz, pc = (z + dz) % nz, (core + dc) % nc
        peers_b.append(((pz * 2 + x_lo, x_hi * (2 * ny) + y * 2 + pc), pz * nc + pc))

    def send(src, dst, s_sem, r_sem, dev):
        pltpu.make_async_remote_copy(
            src_ref=src, dst_ref=dst, send_sem=s_sem, recv_sem=r_sem, device_id=dev, device_id_type=MESH
        ).start()

    def wait_bytes(ref, sem):
        pltpu.make_async_copy(ref, ref, sem).wait()

    barrier = pltpu.get_barrier_semaphore()
    for dev, _ in peers_a + peers_b:
        pl.semaphore_signal(barrier, inc=1, device_id=dev, device_id_type=MESH)

    lane = lax.broadcasted_iota(jnp.int32, (half, LANES), 1)
    first = lane < pts
    lane1 = lax.broadcasted_iota(jnp.int32, (1, LANES), 1)
    first1 = lane1 < pts
    eye = lax.broadcasted_iota(jnp.int32, (LANES, LANES), 0) == lax.broadcasted_iota(
        jnp.int32, (LANES, LANES), 1
    )

    def pack(block):
        return jnp.concatenate([block[:half], block[half:]], axis=1).astype(BF16)

    pack_a[...] = pack(src_ref[...].astype(F32))
    pack_b[...] = pack(tgt_ref[...].astype(F32))

    def own(ref, at):
        line = ref[pl.ds(at // 2, 1), :]
        other = pltpu.roll(line, pts, 1)
        here = at % 2
        low = jnp.where(here == 0, line, other)
        high = jnp.where(here == 0, other, line)
        return jnp.where(first1, low, high)

    gown_a[...] = own(gf_ref, col)
    gown_b[...] = own(gg_ref, row)
    gath_a[me_a] = pack_a[...]
    gath_b[me_b] = pack_b[...]
    gsl_a[me_a] = gown_a[...]
    gsl_b[me_b] = gown_b[...]
    pl.semaphore_wait(barrier, na + nb - 2)

    for dev, _ in peers_b:
        send(pack_b, gath_b.at[me_b], gsem.at[0], gsem.at[1], dev)
    for dev, _ in peers_a:
        send(pack_a, gath_a.at[me_a], gsem.at[2], gsem.at[3], dev)
    for dev, _ in peers_b:
        send(gown_b, gsl_b.at[me_b], gsem.at[4], gsem.at[5], dev)
    for dev, _ in peers_a:
        send(gown_a, gsl_a.at[me_a], gsem.at[6], gsem.at[7], dev)

    def unpack(gath, out, k):
        one, two = gath[2 * k].astype(F32), gath[2 * k + 1].astype(F32)
        at = slice(k * LANES, (k + 1) * LANES)
        low = jnp.where(first, one, pltpu.roll(two, pts, 1))
        high = jnp.where(first, pltpu.roll(one, pts, 1), two)
        out[0:half, at] = low.astype(BF16)
        out[half:feats, at] = high.astype(BF16)
        return jnp.sum(low * low, axis=0, keepdims=True) + jnp.sum(high * high, axis=0, keepdims=True)

    pad = x_ref.shape[0] - feats
    tail_i = (lax.broadcasted_iota(jnp.int32, (pad, ti), 0) == 0).astype(F32).astype(BF16)
    tail_j = (lax.broadcasted_iota(jnp.int32, (pad, tj), 0) == 0).astype(F32).astype(BF16)
    x_ref[feats:, :] = tail_i
    y_ref[feats:, :] = tail_j

    wait_bytes(gath_a.at[pl.ds(0, na - 1)], gsem.at[3])
    sq_i = [unpack(gath_a, x_ref, k) for k in range(ki)]
    wait_bytes(gath_b.at[pl.ds(0, nb - 1)], gsem.at[1])
    sq_j = [unpack(gath_b, y_ref, k) for k in range(kj)]

    def upright(line):
        return jnp.sum(jnp.where(eye, line, 0.0), axis=1, keepdims=True)

    def flat(column):
        return jnp.sum(jnp.where(eye, column, 0.0), axis=0, keepdims=True)

    for k in range(ki):
        row_ref[k : k + 1, :] = sq_i[k]

    def row_lse(at, cols):
        top = None
        for s in range(kj):
            v = c_ref[s, at, :] if cols is None else c_ref[s, at, :] + cols[s]
            top = v if top is None else jnp.maximum(top, v)
        top = jnp.max(top, axis=1, keepdims=True)
        total = None
        for s in range(kj):
            v = c_ref[s, at, :] if cols is None else c_ref[s, at, :] + cols[s]
            e = jnp.exp(v - top)
            total = e if total is None else total + e
        total = jnp.sum(total, axis=1, keepdims=True)
        return top + jnp.log(total)

    def build(k, _):
        base = pl.multiple_of(k * LANES, LANES)
        at = pl.ds(base, LANES)
        cross = lax.dot_general(
            x_ref[0:feats, at], y_ref[0:feats, :], (((0,), (0,)), ((), ())), preferred_element_type=F32
        )
        up = upright(row_ref[pl.ds(k, 1), :])
        for s in range(kj):
            part = cross[:, s * LANES : (s + 1) * LANES]
            c_ref[s, at, :] = -0.25 * ((up + sq_j[s]) - 2.0 * part)
        mine[LR1, pl.ds(k, 1), :] = flat(row_lse(at, None))
        return 0

    lax.fori_loop(0, ki, build, 0)

    def post(i, peers):
        for s, (dev, _) in enumerate(peers):
            send(mine.at[i], slots.at[i, s], ssem.at[i], rsem.at[i], dev)

    def arrive(i, peers):
        n = len(peers)
        wait_bytes(slots.at[i, pl.ds(0, n)], rsem.at[i])
        return [mine[i]] + [slots[i, s] for s in range(n)]

    def tree(parts, op):
        while len(parts) > 1:
            parts = [op(parts[t], parts[t + 1]) if t + 1 < len(parts) else parts[t] for t in range(0, len(parts), 2)]
        return parts[0]

    def add(u, v):
        return u + v

    def lse_round(i, peers):
        post(i, peers)
        parts = arrive(i, peers)
        top = tree(parts, jnp.maximum)
        return -(top + jnp.log(tree([jnp.exp(p - top) for p in parts], add)))

    def sum_round(i, peers):
        post(i, peers)
        return tree(arrive(i, peers), add)

    def raise_rows(vector):
        row_ref[0:ki, :] = vector

        def one(k, _):
            at = pl.ds(pl.multiple_of(k * LANES, LANES), LANES)
            fe_ref[at, :] = jnp.broadcast_to(upright(row_ref[pl.ds(k, 1), :]), (LANES, LANES))
            return 0

        lax.fori_loop(0, ki, one, 0, unroll=2)

    def col_pass(i):
        def one(s, _):
            def highest(k, top):
                at = pl.ds(pl.multiple_of(k * LANES, LANES), LANES)
                v = c_ref[s, at, :] + fe_ref[at, :]
                return jnp.maximum(top, jnp.max(v.reshape(LANES // 8, 8, LANES), axis=0))

            top = lax.fori_loop(0, ki, highest, jnp.full((8, LANES), -jnp.inf, F32), unroll=2)
            top = jnp.max(top, axis=0, keepdims=True)

            def sums(k, total):
                at = pl.ds(pl.multiple_of(k * LANES, LANES), LANES)
                e = jnp.exp(c_ref[s, at, :] + fe_ref[at, :] - top)
                return total + jnp.sum(e.reshape(LANES // 8, 8, LANES), axis=0)

            total = lax.fori_loop(0, ki, sums, jnp.zeros((8, LANES), F32), unroll=2)
            total = jnp.sum(total, axis=0, keepdims=True)
            mine[i, pl.ds(s, 1), :] = top + jnp.log(total)
            return 0

        lax.fori_loop(0, kj, one, 0)

    def lines(vector):
        return [vector[s : s + 1, :] for s in range(vector.shape[0])]

    def row_pass(i, vector):
        cols = lines(vector)

        def one(k, _):
            at = pl.ds(pl.multiple_of(k * LANES, LANES), LANES)
            mine[i, pl.ds(k, 1), :] = flat(row_lse(at, cols))
            return 0

        lax.fori_loop(0, ki, one, 0)

    pot_row = lse_round(LR1, peers_a)
    raise_rows(pot_row)
    col_pass(LC1)
    pot_col = lse_round(LC1, peers_b)
    row_pass(LR2, pot_col)
    pot_row = lse_round(LR2, peers_a)
    raise_rows(pot_row)
    col_pass(LC2)
    pot_col = lse_round(LC2, peers_b)

    cols = lines(pot_col)

    def plan(k, _):
        at = pl.ds(pl.multiple_of(k * LANES, LANES), LANES)
        total = None
        for s in range(kj):
            e = jnp.exp((fe_ref[at, :] + cols[s]) + c_ref[s, at, :]).astype(BF16)
            p_ref[at, s * LANES : (s + 1) * LANES] = e
            e = e.astype(F32)
            total = e if total is None else total + e
        mine[MASS, pl.ds(k, 1), :] = flat(jnp.sum(total, axis=1, keepdims=True))
        return 0

    lax.fori_loop(0, ki, plan, 0)

    def load_lhs(vector, width):
        high = vector.astype(BF16).astype(F32)
        rest = vector - high
        mid = rest.astype(BF16).astype(F32)
        low = rest - mid
        for s in range(width // LANES):
            at = slice(s * LANES, (s + 1) * LANES)
            lhs_ref[0:1, at] = high[s : s + 1, :]
            lhs_ref[1:2, at] = mid[s : s + 1, :]
            lhs_ref[2:3, at] = low[s : s + 1, :]
        return lhs_ref[:, 0:width].astype(BF16)

    def row_dot(i, vector):
        got = lax.dot_general(
            load_lhs(vector, tj), p_ref[...], (((1,), (1,)), ((), ())), preferred_element_type=F32
        )
        got = got[0:1] + got[1:2] + got[2:3]
        for s in range(ki):
            mine[i, s : s + 1, :] = got[:, s * LANES : (s + 1) * LANES]

    def col_dot(i, vector, mass=None):
        got = jnp.dot(load_lhs(vector, ti), p_ref[...], preferred_element_type=F32)
        sums = got[0:1] + got[1:2] + got[2:3]
        for s in range(kj):
            at = slice(s * LANES, (s + 1) * LANES)
            mine[i, s : s + 1, :] = sums[:, at]
            if mass is not None:
                mine[mass, s : s + 1, :] = got[3:4, at]

    lhs_ref[...] = (lax.broadcasted_iota(jnp.int32, lhs_ref.shape, 0) == 3).astype(F32)
    row_mass = sum_round(MASS, peers_a)

    wait_bytes(gsl_a.at[pl.ds(0, na - 1)], gsem.at[7])
    wait_bytes(gsl_b.at[pl.ds(0, nb - 1)], gsem.at[5])
    for k in range(ki):
        row_ref[k : k + 1, :] = jnp.where(first1, gsl_a[2 * k], gsl_a[2 * k + 1])
    grad_f = row_ref[0:ki, :]
    for k in range(kj):
        row_ref[k : k + 1, :] = jnp.where(first1, gsl_b[2 * k], gsl_b[2 * k + 1])
    grad_g = row_ref[0:kj, :]

    col_dot(PULL, grad_f / row_mass, CMASS)
    post(CMASS, peers_b)
    post(PULL, peers_b)
    col_mass = tree(arrive(CMASS, peers_b), add)
    residual = grad_g - tree(arrive(PULL, peers_b), add)

    def line_sum(v):
        return jnp.sum(v, axis=0, keepdims=True)

    def extra_post(i, peers):
        for s, (dev, _) in enumerate(peers):
            send(emine.at[i], eslots.at[i, s], essem.at[i], ersem.at[i], dev)

    def extra_arrive(i, peers):
        n = len(peers)
        wait_bytes(eslots.at[i, pl.ds(0, n)], ersem.at[i])
        got = tree([emine[i]] + [eslots[i, s] for s in range(n)], add)
        return jnp.sum(got, axis=1, keepdims=True)

    emine[...] = jnp.zeros_like(emine)
    dual = pulled_dual = direction = applied = norm = d_c_d = None
    for it in range(CG):
        i_a, i_b = A1 + 2 * it, A1 + 2 * it + 1
        e_a, e_b = 2 * it, 2 * it + 1
        weighted = col_mass * residual
        emine[e_a, 0:1, :] = line_sum(residual * residual)
        emine[e_a, 1:2, :] = line_sum(weighted * residual)
        if it:
            emine[e_a, 2:3, :] = line_sum(weighted * direction)
        extra_post(e_a, peers_a)
        row_dot(i_a, residual)
        post(i_a, peers_a)
        scal = extra_arrive(e_a, peers_a)
        fresh = tree(arrive(i_a, peers_a), add)
        if it:
            beta = scal[0:1] / norm
            direction = residual + beta * direction
            applied = fresh + beta * applied
            d_c_d = scal[1:2] + 2.0 * beta * scal[2:3] + beta * beta * d_c_d
        else:
            direction, applied, d_c_d = residual, fresh, scal[1:2]
        norm = scal[0:1]
        back = applied / row_mass
        emine[e_b, 0:1, :] = line_sum(applied * back)
        extra_post(e_b, peers_b)
        if it < CG - 1:
            col_dot(i_b, back)
            post(i_b, peers_b)
        q_q = extra_arrive(e_b, peers_b)[0:1]
        alpha = norm / ((1.0 + TAU) * d_c_d - q_q)
        dual = alpha * direction if dual is None else dual + alpha * direction
        pulled_dual = alpha * applied if pulled_dual is None else pulled_dual + alpha * applied
        if it < CG - 1:
            image = (1.0 + TAU) * col_mass * direction - tree(arrive(i_b, peers_b), add)
            residual = residual - alpha * image

    dual_row = (grad_f - pulled_dual) / row_mass
    raise_rows(dual_row)
    cols_w = lines(dual)

    acc_ref[...] = jnp.zeros_like(acc_ref)

    def weigh(k, _):
        at = pl.ds(pl.multiple_of(k * LANES, LANES), LANES)
        up = fe_ref[at, :]
        w = jnp.concatenate(
            [
                (p_ref[at, s * LANES : (s + 1) * LANES].astype(F32) * (up + cols_w[s])).astype(BF16)
                for s in range(kj)
            ],
            axis=1,
        )
        acc_ref[...] += jnp.dot(x_ref[:, at], w, preferred_element_type=F32)
        pulled = lax.dot_general(y_ref[...], w, (((1,), (1,)), ((), ())), preferred_element_type=F32)
        spread(x_ref[0:feats, at], pulled, part_a, k)
        return 0

    def spread(points, pulled, part, k):
        grad = 2.0 * (points.astype(F32) * pulled[feats : feats + 1, :] - pulled[0:feats, :])
        low, high = grad[0:half], grad[half:feats]
        part[2 * k] = jnp.where(first, low, pltpu.roll(high, pts, 1)).astype(BF16)
        part[2 * k + 1] = jnp.where(first, pltpu.roll(low, pts, 1), high).astype(BF16)

    lax.fori_loop(0, ki, weigh, 0)
    for k in range(kj):
        at = slice(k * LANES, (k + 1) * LANES)
        spread(y_ref[0:feats, at], acc_ref[:, at], part_b, k)
    for s, (dev, peer) in enumerate(peers_b):
        send(part_b.at[peer], rs_b.at[s], gsem.at[8], gsem.at[9], dev)
    for s, (dev, peer) in enumerate(peers_a):
        send(part_a.at[peer], rs_a.at[s], gsem.at[10], gsem.at[11], dev)

    def collect(part, me, slot, n, sem, out):
        wait_bytes(slot, sem)
        got = tree([part[me].astype(F32)] + [slot[s].astype(F32) for s in range(n)], add)
        out[0:half, :] = got[:, 0:pts]
        out[half:feats, :] = got[:, pts:]

    collect(part_a, me_a, rs_a, na - 1, gsem.at[11], osrc_ref)
    collect(part_b, me_b, rs_b, nb - 1, gsem.at[9], otgt_ref)

    wait_bytes(gath_b.at[pl.ds(0, nb - 1)], gsem.at[0])
    wait_bytes(gath_a.at[pl.ds(0, na - 1)], gsem.at[2])
    wait_bytes(gsl_b.at[pl.ds(0, nb - 1)], gsem.at[4])
    wait_bytes(gsl_a.at[pl.ds(0, na - 1)], gsem.at[6])
    wait_bytes(rs_b, gsem.at[8])
    wait_bytes(rs_a, gsem.at[10])
    group = {i: peers_a for i in (LR1, LR2, MASS, A1, A1 + 2, A1 + 4)}
    for i in range(ROUNDS):
        wait_bytes(slots.at[i, pl.ds(0, len(group.get(i, peers_b)))], ssem.at[i])
    for e in range(2 * CG):
        wait_bytes(eslots.at[e, pl.ds(0, len(peers_a if e % 2 == 0 else peers_b))], essem.at[e])


def body(sizes, src_points, tgt_points, grad_f, grad_g):
    nx, ny, nz, nc = sizes
    feats, pts = src_points.shape
    na, nb = nx * ny, nz * nc
    ti, tj = na * pts, nb * pts
    ki, kj = ti // LANES, tj // LANES
    n = max(na, nb) - 1
    k = max(ki, kj)
    half = feats // 2
    vmem = pl.BlockSpec(memory_space=pltpu.VMEM)
    out = jax.ShapeDtypeStruct((feats, pts), F32)
    return pl.pallas_call(
        functools.partial(kernel, sizes),
        out_shape=(out, out),
        in_specs=[vmem] * 4,
        out_specs=(vmem, vmem),
        scratch_shapes=[
            pltpu.VMEM((half, LANES), BF16),
            pltpu.VMEM((half, LANES), BF16),
            pltpu.VMEM((na, half, LANES), BF16),
            pltpu.VMEM((nb, half, LANES), BF16),
            pltpu.VMEM((1, LANES), F32),
            pltpu.VMEM((1, LANES), F32),
            pltpu.VMEM((na, 1, LANES), F32),
            pltpu.VMEM((nb, 1, LANES), F32),
            pltpu.VMEM((feats + 16, ti), BF16),
            pltpu.VMEM((feats + 16, tj), BF16),
            pltpu.VMEM((kj, ti, LANES), F32),
            pltpu.VMEM((ti, tj), BF16),
            pltpu.VMEM((ti, LANES), F32),
            pltpu.VMEM((8, max(ti, tj)), F32),
            pltpu.VMEM((k, LANES), F32),
            pltpu.VMEM((feats + 16, tj), F32),
            pltpu.VMEM((ROUNDS, k, LANES), F32),
            pltpu.VMEM((ROUNDS, n, k, LANES), F32),
            pltpu.VMEM((2 * CG, 4, LANES), F32),
            pltpu.VMEM((2 * CG, n, 4, LANES), F32),
            pltpu.VMEM((na, half, LANES), BF16),
            pltpu.VMEM((nb, half, LANES), BF16),
            pltpu.VMEM((na - 1, half, LANES), BF16),
            pltpu.VMEM((nb - 1, half, LANES), BF16),
            pltpu.SemaphoreType.DMA((12,)),
            pltpu.SemaphoreType.DMA((ROUNDS,)),
            pltpu.SemaphoreType.DMA((ROUNDS,)),
            pltpu.SemaphoreType.DMA((2 * CG,)),
            pltpu.SemaphoreType.DMA((2 * CG,)),
        ],
        compiler_params=pltpu.CompilerParams(
            collective_id=0, has_side_effects=True, vmem_limit_bytes=40 * 1024 * 1024
        ),
        name="transport",
    )(src_points, tgt_points, grad_f.reshape(-1, LANES), grad_g.reshape(-1, LANES))


def solution(mesh):
    rows, cols = mesh.shape["row"], mesh.shape["col"]
    sizes = (4, cols // 4, rows // 2, 2)
    in_specs = (P(None, ("row", "col")), P(None, ("col", "row")), P("row"), P("col"))
    out_specs = (P(None, ("row", "col")), P(None, ("col", "row")))
    return jax.shard_map(
        functools.partial(body, sizes), mesh=mesh, in_specs=in_specs, out_specs=out_specs, check_vma=False
    )
```

time: 1110 us -> 102 us (0.09)
  blocking collectives: 785 us -> 0 us
  waiting for transfers between devices: 270 us -> 0 us
  Pallas kernels: 0 us -> 97.2 us
  between operations: 21.1 us -> 0.65 us
  matrix products: 18 us -> 0 us
    psum x18 -> x0, blocking collectives: 594 us -> none  [the longest x3 108 us: norm_sum(): return lax.psum(jnp.sum(vector * vector), 'col')]
    psum x2 -> x0, waiting for transfers between devices: 269 us -> none  [the longest x1 154 us: body(): total_src = lax.psum(part_src, 'col')]
    pmax x4 -> x0, blocking collectives: 127 us -> none  [the longest x2 80 us: body(): lax.pmax(lax.map(maxima, (blocks_pts, blocks_sq)).reshape(-1), 'col')]
    pallas_call x0 -> x1, Pallas kernels: none -> 97.2 us  [body(): pl.pallas_call(functools.partial(kernel, sizes), out_shape=(out, out), in...]
    all_gather x2 -> x0, blocking collectives: 63.8 us -> none  [the longest x1 32.1 us: body(): points_row = lax.all_gather(src_points, 'col', axis=1, tiled=True)]
    dot_general x20 -> x0, matrix products: 18 us -> none  [the longest x18 13.7 us: cost_tile(): lax.dot_general(block_pts, points_col, (((0,), (0,)), ((), ())), preferre...]
  transfers between devices with their start and end apart: 2 -> 0, of which waited for: 2 -> 0; matrix products, arithmetic and copies ran while one was open for 0% -> 0% of each run, Pallas kernels for 0% -> 0%
where the time goes in v1:
time: 102 us
  Pallas kernels  97.2 us (95%)
  local copies, waits for them, and re-layouts  4.03 us (4%)
    pallas_call x1, Pallas kernels, body(): pl.pallas_call(functools.partial(kernel, sizes), out_shape=(out, out), in...  97.2 us
    unnamed x10, local copies, waits for them, and re-layouts  4.03 us

profile of v1, /device:TPU:1, one launch (start us, length us, event | category | flops | bytes accessed | tf_op | source)
XLA Modules:
  0.0 101.9 jit_solution(1486524465504734869)
XLA Ops:
  0.6 0.0 copy-start
  0.6 0.7 copy-done
  1.3 0.0 copy-start.1
  1.4 0.7 copy-done.1
  2.1 0.0 copy-start.2
  2.1 0.7 copy-done.2
  2.8 0.0 copy-start.3
  2.8 0.7 copy-done.3
  3.4 97.2 %transport.1 = (f32[64,64]{1,0:T(8,128)S(1)}, f32[64,64]{1,0:T(8,128)S(1)}) custom-call(bf16[64,64]{1,0:T(8,128)(2,1)S(1)} %copy-done, bf16[64,64]{1,0:T(8,128)(2,1)S(1)} %copy-done.1, f32[8,128]{1,0:T(8,128)S(1)} %bitcast.2, f32[8,128]{1,0:T(8,128)S(1)} %bitcast.3), custom_call_target="tpu_custom_call" | custom-call | tf_op jit(solution)/shard_map/transport/pallas_call | solution.py:428
  100.7 0.6 copy.8
  101.3 0.6 copy.9
Async XLA Ops:
  0.6 0.7 copy-start
  1.3 0.7 copy-start.1
  2.1 0.7 copy-start.2
  2.8 0.7 copy-start.3

commit v2 on v1

v2 whole, which is shorter than its diff:
```python
import functools
import math

import jax
import jax.numpy as jnp
from jax import lax
from jax.experimental import pallas as pl
from jax.experimental.pallas import tpu as pltpu
from jax.sharding import PartitionSpec as P

CG = 3
TAU = 0.1
LOG2E = math.log2(math.e)
LANES = 128
MESH = pl.DeviceIdType.MESH
F32 = jnp.float32
BF16 = jnp.bfloat16

LR1, LC1, LR2, LC2, MASS, PULL, CMASS, A1 = range(8)
ROUNDS = 12


def ring(d, n):
    return min(d % n, n - d % n)


def kernel(
    sizes, src_hbm, tgt_hbm, gf_hbm, gg_hbm, osrc_ref, otgt_ref,
    src_ref, tgt_ref, gf_ref, gg_ref,
    pack_a, pack_b, gath_a, gath_b, gown_a, gown_b, gsl_a, gsl_b,
    x_ref, y_ref, c_ref, ct_ref, p_ref, fe_ref, lhs_ref, row_ref, xu_ref, yw_ref, xp_ref, yp_ref,
    mine, slots, emine, eslots, part_a, part_b, rs_a, rs_b,
    isem, gsem, ssem, rsem, essem, ersem, sga, rga, sgb, rgb,
):
    nx, ny, nz, nc = sizes
    na, nb = nx * ny, nz * nc
    row, col = lax.axis_index("row"), lax.axis_index("col")
    z, x_lo = row // 2, row % 2
    x_hi, y, core = col // (2 * ny), (col // 2) % ny, col % 2
    x = x_hi * 2 + x_lo
    me_a, me_b = x * ny + y, z * nc + core
    feats, pts = src_ref.shape
    half = feats // 2
    ti, tj = na * pts, nb * pts
    ki, kj = ti // LANES, tj // LANES

    offs_a = [(i, j) for i in range(nx) for j in range(ny) if i or j]
    offs_a.sort(key=lambda o: -(ring(o[0], nx) + ring(o[1], ny)))
    offs_b = [(i, j) for i in range(nz) for j in range(nc) if i or j]
    offs_b.sort(key=lambda o: -(ring(o[0], nz) + 0.1 * o[1]))
    peers_a, peers_b = [], []
    for dx, dy in offs_a:
        px, py = (x + dx) % nx, (y + dy) % ny
        peers_a.append(((z * 2 + px % 2, (px // 2) * (2 * ny) + py * 2 + core), px * ny + py))
    for dz, dc in offs_b:
        pz, pc = (z + dz) % nz, (core + dc) % nc
        peers_b.append(((pz * 2 + x_lo, x_hi * (2 * ny) + y * 2 + pc), pz * nc + pc))

    def send(src, dst, s_sem, r_sem, dev):
        pltpu.make_async_remote_copy(
            src_ref=src, dst_ref=dst, send_sem=s_sem, recv_sem=r_sem, device_id=dev, device_id_type=MESH
        ).start()

    def wait_bytes(ref, sem):
        pltpu.make_async_copy(ref, ref, sem).wait()

    barrier = pltpu.get_barrier_semaphore()
    for dev, _ in peers_a + peers_b:
        pl.semaphore_signal(barrier, inc=1, device_id=dev, device_id_type=MESH)
    loads = [
        pltpu.make_async_copy(here, there, isem.at[n])
        for n, (here, there) in enumerate(
            ((src_hbm, src_ref), (tgt_hbm, tgt_ref), (gf_hbm, gf_ref), (gg_hbm, gg_ref))
        )
    ]
    for load in loads:
        load.start()

    first = lax.broadcasted_iota(jnp.int32, (half, LANES), 1) < pts
    first1 = lax.broadcasted_iota(jnp.int32, (1, LANES), 1) < pts
    lhs_ref[...] = jnp.zeros_like(lhs_ref)
    emine[...] = jnp.zeros_like(emine)
    for ref in (x_ref, y_ref):
        pad = (ref.shape[0] - feats, ref.shape[1])
        ref[feats:, :] = (lax.broadcasted_iota(jnp.int32, pad, 0) == 0).astype(F32).astype(BF16)

    def pack(block):
        return jnp.concatenate([block[:half], block[half:]], axis=1).astype(BF16)

    def own(ref, at):
        line = ref[pl.ds(at // 2, 1), :]
        other = pltpu.roll(line, pts, 1)
        here = at % 2
        low = jnp.where(here == 0, line, other)
        high = jnp.where(here == 0, other, line)
        return jnp.where(first1, low, high)

    for load in loads:
        load.wait()
    pack_a[...] = pack(src_ref[...].astype(F32))
    pack_b[...] = pack(tgt_ref[...].astype(F32))
    gown_a[...] = own(gf_ref, col)
    gown_b[...] = own(gg_ref, row)
    gath_a[me_a] = pack_a[...]
    gath_b[me_b] = pack_b[...]
    gsl_a[me_a] = gown_a[...]
    gsl_b[me_b] = gown_b[...]
    pl.semaphore_wait(barrier, na + nb - 2)

    for dev, _ in peers_b:
        send(pack_b, gath_b.at[me_b], gsem.at[0], gsem.at[1], dev)
    for dev, _ in peers_a:
        send(pack_a, gath_a.at[me_a], gsem.at[2], gsem.at[3], dev)
    for dev, _ in peers_b:
        send(gown_b, gsl_b.at[me_b], gsem.at[4], gsem.at[5], dev)
    for dev, _ in peers_a:
        send(gown_a, gsl_a.at[me_a], gsem.at[6], gsem.at[7], dev)

    def unpack(gath, out, k):
        one, two = gath[2 * k].astype(F32), gath[2 * k + 1].astype(F32)
        at = slice(k * LANES, (k + 1) * LANES)
        low = jnp.where(first, one, pltpu.roll(two, pts, 1))
        high = jnp.where(first, pltpu.roll(one, pts, 1), two)
        out[0:half, at] = low.astype(BF16)
        out[half:feats, at] = high.astype(BF16)
        return 0.25 * jnp.sum(low * low + high * high, axis=0, keepdims=True)

    wait_bytes(gath_a.at[pl.ds(0, na - 1)], gsem.at[3])
    sq_i = [unpack(gath_a, x_ref, k) for k in range(ki)]
    wait_bytes(gath_b.at[pl.ds(0, nb - 1)], gsem.at[1])
    sq_j = [unpack(gath_b, y_ref, k) for k in range(kj)]

    def upright(line):
        return jnp.broadcast_to(line, (LANES, LANES)).T

    def lanes(k):
        return slice(k * LANES, (k + 1) * LANES)

    def build(out, tall, sq_tall, wide, sq_wide):
        for k, line in enumerate(sq_tall):
            cross = lax.dot_general(
                tall[0:feats, lanes(k)], wide[0:feats, :], (((0,), (0,)), ((), ())), preferred_element_type=F32
            )
            up = upright(line)
            for s, other in enumerate(sq_wide):
                out[s, lanes(k), :] = LOG2E * (0.5 * cross[:, lanes(s)] - (up + other))

    STEP = 16

    def lse_pass(i, tile, vector):
        chunks, height = tile.shape[0], tile.shape[1]
        cols = None if vector is None else lines(vector)
        for k in range(height // LANES):
            tops, sums = [], []
            for h in range(k * LANES, (k + 1) * LANES, STEP):
                vs = [tile[s, h : h + STEP, :] for s in range(chunks)]
                if cols is not None:
                    vs = [v + c for v, c in zip(vs, cols)]
                top = tree(vs, jnp.maximum)
                tops.append(top)
                sums.append(tree([jnp.exp2(v - top) for v in vs], add))
            top = jnp.concatenate(tops, axis=0).T
            total = jnp.concatenate(sums, axis=0).T
            best = jnp.max(top, axis=0, keepdims=True)
            total = jnp.sum(total * jnp.exp2(top - best), axis=0, keepdims=True)
            mine[i, k : k + 1, :] = best + jnp.log2(total)

    def post(i, peers):
        for s, (dev, _) in enumerate(peers):
            send(mine.at[i], slots.at[i, s], ssem.at[i], rsem.at[i], dev)

    def arrive(i, peers):
        n = len(peers)
        wait_bytes(slots.at[i, pl.ds(0, n)], rsem.at[i])
        return [mine[i]] + [slots[i, s] for s in range(n)]

    def tree(parts, op):
        while len(parts) > 1:
            parts = [op(parts[t], parts[t + 1]) if t + 1 < len(parts) else parts[t] for t in range(0, len(parts), 2)]
        return parts[0]

    def add(u, v):
        return u + v

    def lse_end(i, peers):
        parts = arrive(i, peers)
        top = tree(parts, jnp.maximum)
        return -(top + jnp.log2(tree([jnp.exp2(p - top) for p in parts], add)))

    def lines(vector):
        return [vector[s : s + 1, :] for s in range(vector.shape[0])]

    build(c_ref, x_ref, sq_i, y_ref, sq_j)
    lse_pass(LR1, c_ref, None)
    post(LR1, peers_a)
    build(ct_ref, y_ref, sq_j, x_ref, sq_i)
    pot_row = lse_end(LR1, peers_a)
    lse_pass(LC1, ct_ref, pot_row)
    post(LC1, peers_b)
    pot_col = lse_end(LC1, peers_b)
    lse_pass(LR2, c_ref, pot_col)
    post(LR2, peers_a)
    pot_row = lse_end(LR2, peers_a)
    lse_pass(LC2, ct_ref, pot_row)
    post(LC2, peers_b)
    for k, line in enumerate(lines(pot_row)):
        fe_ref[lanes(k), :] = upright(line)
    pot_col = lse_end(LC2, peers_b)

    cols = lines(pot_col)
    for k in range(ki):
        totals = []
        for h in range(k * LANES, (k + 1) * LANES, STEP):
            up = fe_ref[h : h + STEP, :]
            parts = []
            for s in range(kj):
                e = jnp.exp2((up + cols[s]) + c_ref[s, h : h + STEP, :]).astype(BF16)
                p_ref[h : h + STEP, lanes(s)] = e
                parts.append(e.astype(F32))
            totals.append(tree(parts, add))
        mine[MASS, k : k + 1, :] = jnp.sum(jnp.concatenate(totals, axis=0).T, axis=0, keepdims=True)
    post(MASS, peers_a)

    def wide_dot(left):
        return jnp.dot(left, p_ref[...], preferred_element_type=F32)

    def tall_dot(left):
        return lax.dot_general(left, p_ref[...], (((1,), (1,)), ((), ())), preferred_element_type=F32)

    xp_ref[...] = wide_dot(x_ref[...])
    for s in range(kj):
        mine[CMASS, s : s + 1, :] = xp_ref[feats : feats + 1, lanes(s)]
    post(CMASS, peers_b)
    yp_ref[...] = tall_dot(y_ref[...])
    wait_bytes(gsl_a.at[pl.ds(0, na - 1)], gsem.at[7])
    wait_bytes(gsl_b.at[pl.ds(0, nb - 1)], gsem.at[5])
    for k in range(ki):
        row_ref[k : k + 1, :] = jnp.where(first1, gsl_a[2 * k], gsl_a[2 * k + 1])
    grad_f = row_ref[0:ki, :]
    for k in range(kj):
        row_ref[k : k + 1, :] = jnp.where(first1, gsl_b[2 * k], gsl_b[2 * k + 1])
    grad_g = row_ref[0:kj, :]

    def load_lhs(vector, width):
        high = vector.astype(BF16).astype(F32)
        rest = vector - high
        mid = rest.astype(BF16).astype(F32)
        low = rest - mid
        for s in range(width // LANES):
            lhs_ref[0:1, lanes(s)] = high[s : s + 1, :]
            lhs_ref[1:2, lanes(s)] = mid[s : s + 1, :]
            lhs_ref[2:3, lanes(s)] = low[s : s + 1, :]
        return lhs_ref[:, 0:width].astype(BF16)

    def keep(i, got):
        got = got[0:1] + got[1:2] + got[2:3]
        for s in range(got.shape[1] // LANES):
            mine[i, s : s + 1, :] = got[:, lanes(s)]

    def row_dot(i, vector):
        keep(i, tall_dot(load_lhs(vector, tj)))
        post(i, peers_a)

    def col_dot(i, vector):
        keep(i, wide_dot(load_lhs(vector, ti)))
        post(i, peers_b)

    row_mass = tree(arrive(MASS, peers_a), add)
    col_dot(PULL, grad_f / row_mass)
    col_mass = tree(arrive(CMASS, peers_b), add)
    residual = grad_g - tree(arrive(PULL, peers_b), add)

    def line_sum(v):
        return jnp.sum(v, axis=0, keepdims=True)

    def extra_post(i, peers):
        for s, (dev, _) in enumerate(peers):
            send(emine.at[i], eslots.at[i, s], essem.at[i], ersem.at[i], dev)

    def extra_arrive(i, peers):
        n = len(peers)
        wait_bytes(eslots.at[i, pl.ds(0, n)], ersem.at[i])
        got = tree([emine[i]] + [eslots[i, s] for s in range(n)], add)
        return jnp.sum(got, axis=1, keepdims=True)

    def spread(points, pulled, part, k):
        grad = 2.0 * (points.astype(F32) * pulled[feats : feats + 1, :] - pulled[0:feats, :])
        low, high = grad[0:half], grad[half:feats]
        part[2 * k] = jnp.where(first, low, pltpu.roll(high, pts, 1)).astype(BF16)
        part[2 * k + 1] = jnp.where(first, pltpu.roll(low, pts, 1), high).astype(BF16)

    def split(out, points, factors):
        rows = points.shape[0]
        for s, factor in enumerate(factors):
            v = points[:, lanes(s)].astype(F32) * factor
            high = v.astype(BF16)
            out[0:rows, lanes(s)] = high
            out[rows : 2 * rows, lanes(s)] = (v - high.astype(F32)).astype(BF16)

    rows = feats + 16

    def gradients(g, on_row, on_col):
        us, ws = lines(on_row), lines(on_col)
        split(yw_ref, y_ref, ws)
        got = tall_dot(yw_ref[...])
        split(xu_ref, x_ref, us)
        for k in range(ki):
            pulled = got[0:rows, lanes(k)] + got[rows:, lanes(k)] + us[k] * yp_ref[:, lanes(k)]
            spread(x_ref[0:feats, lanes(k)], pulled, part_a.at[g], k)
        for s, (dev, peer) in enumerate(peers_a):
            send(part_a.at[g, peer], rs_a.at[g, s], sga.at[g], rga.at[g], dev)
        got = wide_dot(xu_ref[...])
        for k in range(kj):
            pulled = got[0:rows, lanes(k)] + got[rows:, lanes(k)] + ws[k] * xp_ref[:, lanes(k)]
            spread(y_ref[0:feats, lanes(k)], pulled, part_b.at[g], k)
        for s, (dev, peer) in enumerate(peers_b):
            send(part_b.at[g, peer], rs_b.at[g, s], sgb.at[g], rgb.at[g], dev)

    dual = pulled_dual = direction = applied = norm = d_c_d = None
    for it in range(CG):
        i_a, i_b = A1 + 2 * it, A1 + 2 * it + 1
        e_a, e_b = 2 * it, 2 * it + 1
        weighted = col_mass * residual
        emine[e_a, 0:1, :] = line_sum(residual * residual)
        emine[e_a, 1:2, :] = line_sum(weighted * residual)
        if it:
            emine[e_a, 2:3, :] = line_sum(weighted * direction)
        extra_post(e_a, peers_a)
        row_dot(i_a, residual)
        if it == CG - 1:
            gradients(0, (grad_f - pulled_dual) / row_mass, dual)
        scal = extra_arrive(e_a, peers_a)
        fresh = tree(arrive(i_a, peers_a), add)
        if it:
            beta = scal[0:1] / norm
            direction = residual + beta * direction
            applied = fresh + beta * applied
            d_c_d = scal[1:2] + 2.0 * beta * scal[2:3] + beta * beta * d_c_d
        else:
            direction, applied, d_c_d = residual, fresh, scal[1:2]
        norm = scal[0:1]
        back = applied / row_mass
        emine[e_b, 0:1, :] = line_sum(applied * back)
        extra_post(e_b, peers_b)
        if it == CG - 1:
            gradients(1, -back, direction)
            q_q = extra_arrive(e_b, peers_b)[0:1]
            alpha = norm / ((1.0 + TAU) * d_c_d - q_q)
            continue
        col_dot(i_b, back)
        q_q = extra_arrive(e_b, peers_b)[0:1]
        alpha = norm / ((1.0 + TAU) * d_c_d - q_q)
        dual = alpha * direction if it == 0 else dual + alpha * direction
        pulled_dual = alpha * applied if it == 0 else pulled_dual + alpha * applied
        image = (1.0 + TAU) * col_mass * direction - tree(arrive(i_b, peers_b), add)
        residual = residual - alpha * image

    def collect(g, part, me, slot, n, sem):
        wait_bytes(slot.at[g], sem.at[g])
        return tree([part[g, me].astype(F32)] + [slot[g, s].astype(F32) for s in range(n)], add)

    def store(out, got):
        out[0:half, :] = got[:, 0:pts]
        out[half:feats, :] = got[:, pts:]

    base_a = collect(0, part_a, me_a, rs_a, na - 1, rga)
    base_b = collect(0, part_b, me_b, rs_b, nb - 1, rgb)
    store(osrc_ref, base_a + alpha * collect(1, part_a, me_a, rs_a, na - 1, rga))
    store(otgt_ref, base_b + alpha * collect(1, part_b, me_b, rs_b, nb - 1, rgb))

    wait_bytes(gath_b.at[pl.ds(0, nb - 1)], gsem.at[0])
    wait_bytes(gath_a.at[pl.ds(0, na - 1)], gsem.at[2])
    wait_bytes(gsl_b.at[pl.ds(0, nb - 1)], gsem.at[4])
    wait_bytes(gsl_a.at[pl.ds(0, na - 1)], gsem.at[6])
    for g in range(2):
        wait_bytes(rs_a.at[g], sga.at[g])
        wait_bytes(rs_b.at[g], sgb.at[g])
    over_a = (LR1, LR2, MASS, A1, A1 + 2, A1 + 4)
    for i in range(ROUNDS):
        wait_bytes(slots.at[i, pl.ds(0, len(peers_a if i in over_a else peers_b))], ssem.at[i])
    for e in range(2 * CG):
        wait_bytes(eslots.at[e, pl.ds(0, len(peers_a if e % 2 == 0 else peers_b))], essem.at[e])


def body(sizes, src_points, tgt_points, grad_f, grad_g):
    nx, ny, nz, nc = sizes
    feats, pts = src_points.shape
    na, nb = nx * ny, nz * nc
    ti, tj = na * pts, nb * pts
    ki, kj = ti // LANES, tj // LANES
    n = max(na, nb) - 1
    k = max(ki, kj)
    half = feats // 2
    rows = feats + 16
    vmem = pl.BlockSpec(memory_space=pltpu.VMEM)
    out = jax.ShapeDtypeStruct((feats, pts), F32)
    return pl.pallas_call(
        functools.partial(kernel, sizes),
        out_shape=(out, out),
        in_specs=[pl.BlockSpec(memory_space=pl.ANY)] * 4,
        out_specs=(vmem, vmem),
        scratch_shapes=[
            pltpu.VMEM((feats, pts), BF16),
            pltpu.VMEM((feats, pts), BF16),
            pltpu.VMEM((grad_f.shape[0] // LANES, LANES), F32),
            pltpu.VMEM((grad_g.shape[0] // LANES, LANES), F32),
            pltpu.VMEM((half, LANES), BF16),
            pltpu.VMEM((half, LANES), BF16),
            pltpu.VMEM((na, half, LANES), BF16),
            pltpu.VMEM((nb, half, LANES), BF16),
            pltpu.VMEM((1, LANES), F32),
            pltpu.VMEM((1, LANES), F32),
            pltpu.VMEM((na, 1, LANES), F32),
            pltpu.VMEM((nb, 1, LANES), F32),
            pltpu.VMEM((rows, ti), BF16),
            pltpu.VMEM((rows, tj), BF16),
            pltpu.VMEM((kj, ti, LANES), F32),
            pltpu.VMEM((ki, tj, LANES), F32),
            pltpu.VMEM((ti, tj), BF16),
            pltpu.VMEM((ti, LANES), F32),
            pltpu.VMEM((8, max(ti, tj)), F32),
            pltpu.VMEM((k, LANES), F32),
            pltpu.VMEM((2 * rows, ti), BF16),
            pltpu.VMEM((2 * rows, tj), BF16),
            pltpu.VMEM((rows, tj), F32),
            pltpu.VMEM((rows, ti), F32),
            pltpu.VMEM((ROUNDS, k, LANES), F32),
            pltpu.VMEM((ROUNDS, n, k, LANES), F32),
            pltpu.VMEM((2 * CG, 4, LANES), F32),
            pltpu.VMEM((2 * CG, n, 4, LANES), F32),
            pltpu.VMEM((2, na, half, LANES), BF16),
            pltpu.VMEM((2, nb, half, LANES), BF16),
            pltpu.VMEM((2, na - 1, half, LANES), BF16),
            pltpu.VMEM((2, nb - 1, half, LANES), BF16),
            pltpu.SemaphoreType.DMA((4,)),
            pltpu.SemaphoreType.DMA((8,)),
            pltpu.SemaphoreType.DMA((ROUNDS,)),
            pltpu.SemaphoreType.DMA((ROUNDS,)),
            pltpu.SemaphoreType.DMA((2 * CG,)),
            pltpu.SemaphoreType.DMA((2 * CG,)),
            pltpu.SemaphoreType.DMA((2,)),
            pltpu.SemaphoreType.DMA((2,)),
            pltpu.SemaphoreType.DMA((2,)),
            pltpu.SemaphoreType.DMA((2,)),
        ],
        compiler_params=pltpu.CompilerParams(
            collective_id=0, has_side_effects=True, vmem_limit_bytes=40 * 1024 * 1024
        ),
        name="transport",
    )(src_points, tgt_points, grad_f.reshape(-1, LANES), grad_g.reshape(-1, LANES))


def solution(mesh):
    rows, cols = mesh.shape["row"], mesh.shape["col"]
    sizes = (4, cols // 4, rows // 2, 2)
    in_specs = (P(None, ("row", "col")), P(None, ("col", "row")), P("row"), P("col"))
    out_specs = (P(None, ("row", "col")), P(None, ("col", "row")))
    return jax.shard_map(
        functools.partial(body, sizes), mesh=mesh, in_specs=in_specs, out_specs=out_specs, check_vma=False
    )
```

time: 102 us -> 88.4 us (0.87)
  Pallas kernels: 97.2 us -> 83.4 us
    pallas_call x1, Pallas kernels: 97.2 us -> 83.4 us  [body(): pl.pallas_call(functools.partial(kernel, sizes), out_shape=(out, out), in...]
where the time goes in v2:
time: 88.4 us; the launch traced here: 88.1 us
  Pallas kernels  83.4 us (94%)
  local copies, waits for them, and re-layouts  4.03 us (5%)
    pallas_call x1, Pallas kernels, body(): pl.pallas_call(functools.partial(kernel, sizes), out_shape=(out, out), in...  83.4 us
    unnamed x10, local copies, waits for them, and re-layouts  4.03 us

profile of v2, /device:TPU:1, one launch (start us, length us, event | category | flops | bytes accessed | tf_op | source)
XLA Modules:
  0.0 88.1 jit_solution(8882205368658467052)
XLA Ops:
  0.6 0.0 copy-start
  0.6 0.7 copy-done
  1.3 0.0 copy-start.1
  1.4 0.7 copy-done.1
  2.1 0.0 copy-start.2
  2.1 0.7 copy-done.2
  2.8 0.0 copy-start.3
  2.8 0.7 copy-done.3
  3.4 83.4 %transport.1 = (f32[64,64]{1,0:T(8,128)S(1)}, f32[64,64]{1,0:T(8,128)S(1)}) custom-call(bf16[64,64]{1,0:T(8,128)(2,1)S(1)} %copy-done, bf16[64,64]{1,0:T(8,128)(2,1)S(1)} %copy-done.1, f32[8,128]{1,0:T(8,128)S(1)} %bitcast.2, f32[8,128]{1,0:T(8,128)S(1)} %bitcast.3), custom_call_target="tpu_custom_call" | custom-call | tf_op jit(solution)/shard_map/transport/pallas_call | solution.py:397
  86.8 0.6 copy.8
  87.5 0.6 copy.9
Async XLA Ops:
  0.6 0.7 copy-start
  1.3 0.7 copy-start.1
  2.1 0.7 copy-start.2
  2.8 0.7 copy-start.3

commit v3 on v2

--- a/solution.py
+++ b/solution.py
@@ -28,7 +28,7 @@
     sizes, src_hbm, tgt_hbm, gf_hbm, gg_hbm, osrc_ref, otgt_ref,
     src_ref, tgt_ref, gf_ref, gg_ref,
     pack_a, pack_b, gath_a, gath_b, gown_a, gown_b, gsl_a, gsl_b,
-    x_ref, y_ref, c_ref, ct_ref, p_ref, fe_ref, lhs_ref, row_ref, xu_ref, yw_ref, xp_ref, yp_ref,
+    x_ref, y_ref, c_ref, ct_ref, p_ref, fe_ref, lhs_ref, row_ref, xu_ref, yw_ref, xp_ref, yp_ref, yk_ref,
     mine, slots, emine, eslots, part_a, part_b, rs_a, rs_b,
     isem, gsem, ssem, rsem, essem, ersem, sga, rga, sgb, rgb,
 ):
@@ -299,22 +299,43 @@
 
     rows = feats + 16
 
-    def gradients(g, on_row, on_col):
-        us, ws = lines(on_row), lines(on_col)
-        split(yw_ref, y_ref, ws)
-        got = tall_dot(yw_ref[...])
+    def tgt_parts(g, us, ws, between):
         split(xu_ref, x_ref, us)
-        for k in range(ki):
-            pulled = got[0:rows, lanes(k)] + got[rows:, lanes(k)] + us[k] * yp_ref[:, lanes(k)]
-            spread(x_ref[0:feats, lanes(k)], pulled, part_a.at[g], k)
-        for s, (dev, peer) in enumerate(peers_a):
-            send(part_a.at[g, peer], rs_a.at[g, s], sga.at[g], rga.at[g], dev)
         got = wide_dot(xu_ref[...])
+        between()
         for k in range(kj):
             pulled = got[0:rows, lanes(k)] + got[rows:, lanes(k)] + ws[k] * xp_ref[:, lanes(k)]
             spread(y_ref[0:feats, lanes(k)], pulled, part_b.at[g], k)
         for s, (dev, peer) in enumerate(peers_b):
             send(part_b.at[g, peer], rs_b.at[g, s], sgb.at[g], rgb.at[g], dev)
+
+    def src_parts(g, us, pulled_of):
+        for k in range(ki):
+            spread(x_ref[0:feats, lanes(k)], pulled_of(k) + us[k] * yp_ref[:, lanes(k)], part_a.at[g], k)
+        for s, (dev, peer) in enumerate(peers_a):
+            send(part_a.at[g, peer], rs_a.at[g, s], sga.at[g], rga.at[g], dev)
+
+    def early_gradients(on_row, on_col, residual, direction):
+        us, ws = lines(on_row), lines(on_col)
+        for t, vector in enumerate((on_col, residual, direction)):
+            split(yw_ref.at[pl.ds(2 * rows * t, 2 * rows)], y_ref, lines(vector))
+        got = tall_dot(yw_ref[...])
+        for t in range(1, 3):
+            at = 2 * rows * t
+            yk_ref[t - 1] = got[at : at + rows] + got[at + rows : at + 2 * rows]
+
+        def between():
+            src_parts(0, us, lambda k: got[0:rows, lanes(k)] + got[rows : 2 * rows, lanes(k)])
+
+        tgt_parts(0, us, ws, between)
+
+    def late_gradients(on_row, on_col, beta):
+        us, ws = lines(on_row), lines(on_col)
+
+        def between():
+            src_parts(1, us, lambda k: yk_ref[0, :, lanes(k)] + beta * yk_ref[1, :, lanes(k)])
+
+        tgt_parts(1, us, ws, between)
 
     dual = pulled_dual = direction = applied = norm = d_c_d = None
     for it in range(CG):
@@ -328,7 +349,7 @@
         extra_post(e_a, peers_a)
         row_dot(i_a, residual)
         if it == CG - 1:
-            gradients(0, (grad_f - pulled_dual) / row_mass, dual)
+            early_gradients((grad_f - pulled_dual) / row_mass, dual, residual, direction)
         scal = extra_arrive(e_a, peers_a)
         fresh = tree(arrive(i_a, peers_a), add)
         if it:
@@ -343,7 +364,7 @@
         emine[e_b, 0:1, :] = line_sum(applied * back)
         extra_post(e_b, peers_b)
         if it == CG - 1:
-            gradients(1, -back, direction)
+            late_gradients(-back, direction, beta)
             q_q = extra_arrive(e_b, peers_b)[0:1]
             alpha = norm / ((1.0 + TAU) * d_c_d - q_q)
             continue
@@ -421,9 +442,10 @@
             pltpu.VMEM((8, max(ti, tj)), F32),
             pltpu.VMEM((k, LANES), F32),
             pltpu.VMEM((2 * rows, ti), BF16),
-            pltpu.VMEM((2 * rows, tj), BF16),
+            pltpu.VMEM((6 * rows, tj), BF16),
             pltpu.VMEM((rows, tj), F32),
             pltpu.VMEM((rows, ti), F32),
+            pltpu.VMEM((2, rows, ti), F32),
             pltpu.VMEM((ROUNDS, k, LANES), F32),
             pltpu.VMEM((ROUNDS, n, k, LANES), F32),
             pltpu.VMEM((2 * CG, 4, LANES), F32),
@@ -449,7 +471,6 @@
         name="transport",
     )(src_points, tgt_points, grad_f.reshape(-1, LANES), grad_g.reshape(-1, LANES))
 
-
 def solution(mesh):
     rows, cols = mesh.shape["row"], mesh.shape["col"]
     sizes = (4, cols // 4, rows // 2, 2)

time: 88.4 us -> 87.8 us (level)
  no operation moved by 1% of the time
where the time goes in v3:
time: 87.8 us; the launch traced here: 87.5 us
  Pallas kernels  82.8 us (94%)
  local copies, waits for them, and re-layouts  4.03 us (5%)
    pallas_call x1, Pallas kernels, body(): pl.pallas_call(functools.partial(kernel, sizes), out_shape=(out, out), in...  82.8 us
    unnamed x10, local copies, waits for them, and re-layouts  4.03 us

profile of v3, /device:TPU:1, one launch (start us, length us, event | category | flops | bytes accessed | tf_op | source)
XLA Modules:
  0.0 87.5 jit_solution(7294526344950181240)
XLA Ops:
  0.6 0.0 copy-start
  0.6 0.7 copy-done
  1.3 0.0 copy-start.1
  1.4 0.7 copy-done.1
  2.1 0.0 copy-start.2
  2.1 0.7 copy-done.2
  2.8 0.0 copy-start.3
  2.8 0.7 copy-done.3
  3.4 82.8 %transport.1 = (f32[64,64]{1,0:T(8,128)S(1)}, f32[64,64]{1,0:T(8,128)S(1)}) custom-call(bf16[64,64]{1,0:T(8,128)(2,1)S(1)} %copy-done, bf16[64,64]{1,0:T(8,128)(2,1)S(1)} %copy-done.1, f32[8,128]{1,0:T(8,128)S(1)} %bitcast.2, f32[8,128]{1,0:T(8,128)S(1)} %bitcast.3), custom_call_target="tpu_custom_call" | custom-call | tf_op jit(solution)/shard_map/transport/pallas_call | solution.py:418
  86.3 0.6 copy.8
  86.9 0.6 copy.9
Async XLA Ops:
  0.6 0.7 copy-start
  1.3 0.7 copy-start.1
  2.1 0.7 copy-start.2
  2.8 0.7 copy-start.3

commit v4 on v3

--- a/solution.py
+++ b/solution.py
@@ -403,6 +403,11 @@
         wait_bytes(eslots.at[e, pl.ds(0, len(peers_a if e % 2 == 0 else peers_b))], essem.at[e])
 
 
+def hand_over(one_ref, two_ref, first_ref, second_ref):
+    first_ref[...] = one_ref[...]
+    second_ref[...] = two_ref[...]
+
+
 def body(sizes, src_points, tgt_points, grad_f, grad_g):
     nx, ny, nz, nc = sizes
     feats, pts = src_points.shape
@@ -415,7 +420,7 @@
     rows = feats + 16
     vmem = pl.BlockSpec(memory_space=pltpu.VMEM)
     out = jax.ShapeDtypeStruct((feats, pts), F32)
-    return pl.pallas_call(
+    both = pl.pallas_call(
         functools.partial(kernel, sizes),
         out_shape=(out, out),
         in_specs=[pl.BlockSpec(memory_space=pl.ANY)] * 4,
@@ -466,10 +471,14 @@
             pltpu.SemaphoreType.DMA((2,)),
         ],
         compiler_params=pltpu.CompilerParams(
-            collective_id=0, has_side_effects=True, vmem_limit_bytes=40 * 1024 * 1024
+            collective_id=0, has_side_effects=True, vmem_limit_bytes=56 * 1024 * 1024
         ),
         name="transport",
     )(src_points, tgt_points, grad_f.reshape(-1, LANES), grad_g.reshape(-1, LANES))
+    return pl.pallas_call(
+        hand_over, out_shape=(out, out), in_specs=[vmem] * 2, out_specs=(vmem, vmem), name="hand_over"
+    )(*both)
+
 
 def solution(mesh):
     rows, cols = mesh.shape["row"], mesh.shape["col"]

time: 87.8 us -> 86.1 us (0.981)
  local copies, waits for them, and re-layouts: 4.03 us -> 0 us
  Pallas kernels: 82.8 us -> 85.3 us
    unnamed x10 -> x0, local copies, waits for them, and re-layouts: 4.03 us -> none
    pallas_call x0 -> x1, Pallas kernels: none -> 1.4 us  [body(): pl.pallas_call(hand_over, out_shape=(out, out), in_specs=[vmem] * 2, out_...]
    pallas_call x1, Pallas kernels: 82.8 us -> 83.9 us  [body(): pl.pallas_call(functools.partial(kernel, sizes), out_shape=(out, out), in...]
where the time goes in v4:
time: 86.1 us; the launch traced here: 85.9 us
  Pallas kernels  85.3 us (99%)
    pallas_call x1, Pallas kernels, body(): pl.pallas_call(functools.partial(kernel, sizes), out_shape=(out, out), in...  83.9 us

profile of v4, /device:TPU:1, one launch (start us, length us, event | category | flops | bytes accessed | tf_op | source)
XLA Modules:
  0.0 85.9 jit_solution(15902599337726699565)
XLA Ops:
  0.6 83.9 %transport.1 = (f32[64,64]{1,0:T(8,128)}, f32[64,64]{1,0:T(8,128)}) custom-call(bf16[64,64]{1,0:T(8,128)(2,1)} %src_hbm.1, bf16[64,64]{1,0:T(8,128)(2,1)} %tgt_hbm.1, f32[8,128]{1,0:T(8,128)} %bitcast.2, f32[8,128]{1,0:T(8,128)} %bitcast.3), custom_call_target="tpu_custom_call" | custom-call | tf_op jit(solution)/shard_map/transport/pallas_call | solution.py:423
  84.5 1.4 %hand_over.1 = (f32[64,64]{1,0:T(8,128)}, f32[64,64]{1,0:T(8,128)}) custom-call(f32[64,64]{1,0:T(8,128)} %get-tuple-element.4.one_ref, f32[64,64]{1,0:T(8,128)} %get-tuple-element.5.two_ref), custom_call_target="tpu_custom_call" | custom-call | tf_op jit(solution)/shard_map/hand_over/pallas_call | solution.py:478

commit v5 on v4

--- a/solution.py
+++ b/solution.py
@@ -29,14 +29,14 @@
     src_ref, tgt_ref, gf_ref, gg_ref,
     pack_a, pack_b, gath_a, gath_b, gown_a, gown_b, gsl_a, gsl_b,
     x_ref, y_ref, c_ref, ct_ref, p_ref, fe_ref, lhs_ref, row_ref, xu_ref, yw_ref, xp_ref, yp_ref, yk_ref,
-    mine, slots, emine, eslots, part_a, part_b, rs_a, rs_b,
-    isem, gsem, ssem, rsem, essem, ersem, sga, rga, sgb, rgb,
+    mine, slots, hmine, hslots, top_ref, sum_ref, emine, eslots, part_a, part_b, rs_a, rs_b,
+    isem, gsem, hsem, hrsem, ssem, rsem, essem, ersem, sga, rga, sgb, rgb,
 ):
     nx, ny, nz, nc = sizes
     na, nb = nx * ny, nz * nc
     row, col = lax.axis_index("row"), lax.axis_index("col")
-    z, x_lo = row // 2, row % 2
-    x_hi, y, core = col // (2 * ny), (col // 2) % ny, col % 2
+    z, x_lo = lax.div(row, 2), lax.rem(row, 2)
+    x_hi, y, core = lax.div(col, 2 * ny), lax.rem(lax.div(col, 2), ny), lax.rem(col, 2)
     x = x_hi * 2 + x_lo
     me_a, me_b = x * ny + y, z * nc + core
     feats, pts = src_ref.shape
@@ -49,12 +49,16 @@
     offs_b = [(i, j) for i in range(nz) for j in range(nc) if i or j]
     offs_b.sort(key=lambda o: -(ring(o[0], nz) + 0.1 * o[1]))
     peers_a, peers_b = [], []
+    xs = [lax.rem(x + d, nx) for d in range(nx)]
+    xs = [(z * 2 + lax.rem(p, 2), lax.div(p, 2) * (2 * ny) + core, p * ny) for p in xs]
+    ys = [lax.rem(y + d, ny) for d in range(ny)]
+    zs = [lax.rem(z + d, nz) for d in range(nz)]
+    zs = [(p * 2 + x_lo, p * nc) for p in zs]
+    cs = [(col - core + p, p) for p in (core, 1 - core)]
     for dx, dy in offs_a:
-        px, py = (x + dx) % nx, (y + dy) % ny
-        peers_a.append(((z * 2 + px % 2, (px // 2) * (2 * ny) + py * 2 + core), px * ny + py))
+        peers_a.append(((xs[dx][0], xs[dx][1] + ys[dy] * 2), xs[dx][2] + ys[dy]))
     for dz, dc in offs_b:
-        pz, pc = (z + dz) % nz, (core + dc) % nc
-        peers_b.append(((pz * 2 + x_lo, x_hi * (2 * ny) + y * 2 + pc), pz * nc + pc))
+        peers_b.append(((zs[dz][0], cs[dc][0]), zs[dz][1] + cs[dc][1]))
 
     def send(src, dst, s_sem, r_sem, dev):
         pltpu.make_async_remote_copy(
@@ -65,7 +69,7 @@
         pltpu.make_async_copy(ref, ref, sem).wait()
 
     barrier = pltpu.get_barrier_semaphore()
-    for dev, _ in peers_a + peers_b:
+    for dev, _ in peers_b + peers_a:
         pl.semaphore_signal(barrier, inc=1, device_id=dev, device_id_type=MESH)
     loads = [
         pltpu.make_async_copy(here, there, isem.at[n])
@@ -88,9 +92,9 @@
         return jnp.concatenate([block[:half], block[half:]], axis=1).astype(BF16)
 
     def own(ref, at):
-        line = ref[pl.ds(at // 2, 1), :]
+        line = ref[pl.ds(lax.div(at, 2), 1), :]
         other = pltpu.roll(line, pts, 1)
-        here = at % 2
+        here = lax.rem(at, 2)
         low = jnp.where(here == 0, line, other)
         high = jnp.where(here == 0, other, line)
         return jnp.where(first1, low, high)
@@ -123,7 +127,7 @@
         high = jnp.where(first, pltpu.roll(one, pts, 1), two)
         out[0:half, at] = low.astype(BF16)
         out[half:feats, at] = high.astype(BF16)
-        return 0.25 * jnp.sum(low * low + high * high, axis=0, keepdims=True)
+        return (0.25 * LOG2E) * jnp.sum(low * low + high * high, axis=0, keepdims=True)
 
     wait_bytes(gath_a.at[pl.ds(0, na - 1)], gsem.at[3])
     sq_i = [unpack(gath_a, x_ref, k) for k in range(ki)]
@@ -143,27 +147,46 @@
             )
             up = upright(line)
             for s, other in enumerate(sq_wide):
-                out[s, lanes(k), :] = LOG2E * (0.5 * cross[:, lanes(s)] - (up + other))
+                out[s, lanes(k), :] = (0.5 * LOG2E) * cross[:, lanes(s)] - (up + other)
 
     STEP = 16
 
-    def lse_pass(i, tile, vector):
-        chunks, height = tile.shape[0], tile.shape[1]
-        cols = None if vector is None else lines(vector)
-        for k in range(height // LANES):
+    def steps(k):
+        return [slice(h, h + STEP) for h in range(k * LANES, (k + 1) * LANES, STEP)]
+
+    def lse_start(tile, cols):
+        for k in range(tile.shape[1] // LANES):
+            for at in steps(k):
+                vs = [tile[s, at, :] + c for s, c in enumerate(cols)]
+                top = tree(vs, jnp.maximum)
+                top_ref[at, :] = top
+                sum_ref[at, :] = tree([jnp.exp2(v - top) for v in vs], add)
+
+    def lse_finish(i, tile, cols, peers):
+        chunks, blocks = tile.shape[0], tile.shape[1] // LANES
+        for k in range(blocks):
             tops, sums = [], []
-            for h in range(k * LANES, (k + 1) * LANES, STEP):
-                vs = [tile[s, h : h + STEP, :] for s in range(chunks)]
-                if cols is not None:
-                    vs = [v + c for v, c in zip(vs, cols)]
-                top = tree(vs, jnp.maximum)
+            for at in steps(k):
+                if cols is None:
+                    vs = [tile[s, at, :] for s in range(chunks)]
+                    top = tree(vs, jnp.maximum)
+                    total = tree([jnp.exp2(v - top) for v in vs], add)
+                else:
+                    vs = [tile[chunks - len(cols) + s, at, :] + c for s, c in enumerate(cols)]
+                    before = top_ref[at, :]
+                    top = jnp.maximum(before, tree(vs, jnp.maximum))
+                    total = tree([jnp.exp2(v - top) for v in vs] + [sum_ref[at, :] * jnp.exp2(before - top)], add)
                 tops.append(top)
-                sums.append(tree([jnp.exp2(v - top) for v in vs], add))
+                sums.append(total)
             top = jnp.concatenate(tops, axis=0).T
             total = jnp.concatenate(sums, axis=0).T
             best = jnp.max(top, axis=0, keepdims=True)
             total = jnp.sum(total * jnp.exp2(top - best), axis=0, keepdims=True)
-            mine[i, k : k + 1, :] = best + jnp.log2(total)
+            part, line = k // (blocks // 2), k % (blocks // 2)
+            hmine[i, part, line : line + 1, :] = best + jnp.log2(total)
+            if line == blocks // 2 - 1:
+                for s, (dev, _) in enumerate(peers):
+                    send(hmine.at[i, part], hslots.at[i, part, s], hsem.at[i, part], hrsem.at[i, part], dev)
 
     def post(i, peers):
         for s, (dev, _) in enumerate(peers):
@@ -182,43 +205,49 @@
     def add(u, v):
         return u + v
 
-    def lse_end(i, peers):
-        parts = arrive(i, peers)
+    def half_end(i, part, peers):
+        n = len(peers)
+        wait_bytes(hslots.at[i, part, pl.ds(0, n)], hrsem.at[i, part])
+        parts = [hmine[i, part]] + [hslots[i, part, s] for s in range(n)]
         top = tree(parts, jnp.maximum)
-        return -(top + jnp.log2(tree([jnp.exp2(p - top) for p in parts], add)))
+        return lines(-(top + jnp.log2(tree([jnp.exp2(p - top) for p in parts], add))))
 
     def lines(vector):
         return [vector[s : s + 1, :] for s in range(vector.shape[0])]
 
     build(c_ref, x_ref, sq_i, y_ref, sq_j)
-    lse_pass(LR1, c_ref, None)
-    post(LR1, peers_a)
+    lse_finish(LR1, c_ref, None, peers_a)
     build(ct_ref, y_ref, sq_j, x_ref, sq_i)
-    pot_row = lse_end(LR1, peers_a)
-    lse_pass(LC1, ct_ref, pot_row)
-    post(LC1, peers_b)
-    pot_col = lse_end(LC1, peers_b)
-    lse_pass(LR2, c_ref, pot_col)
-    post(LR2, peers_a)
-    pot_row = lse_end(LR2, peers_a)
-    lse_pass(LC2, ct_ref, pot_row)
-    post(LC2, peers_b)
-    for k, line in enumerate(lines(pot_row)):
+    for i, tile, here, there in (
+        (LC1, ct_ref, peers_a, peers_b),
+        (LR2, c_ref, peers_b, peers_a),
+        (LC2, ct_ref, peers_a, peers_b),
+    ):
+        one = half_end(i - 1, 0, here)
+        lse_start(tile, one)
+        two = half_end(i - 1, 1, here)
+        lse_finish(i, tile, two, there)
+    for k, line in enumerate(one + two):
         fe_ref[lanes(k), :] = upright(line)
-    pot_col = lse_end(LC2, peers_b)
-
-    cols = lines(pot_col)
-    for k in range(ki):
-        totals = []
-        for h in range(k * LANES, (k + 1) * LANES, STEP):
-            up = fe_ref[h : h + STEP, :]
-            parts = []
-            for s in range(kj):
-                e = jnp.exp2((up + cols[s]) + c_ref[s, h : h + STEP, :]).astype(BF16)
-                p_ref[h : h + STEP, lanes(s)] = e
-                parts.append(e.astype(F32))
-            totals.append(tree(parts, add))
-        mine[MASS, k : k + 1, :] = jnp.sum(jnp.concatenate(totals, axis=0).T, axis=0, keepdims=True)
+
+    for part in range(2):
+        cols = half_end(LC2, part, peers_b)
+        at_col = part * len(cols)
+        for k in range(ki):
+            totals = []
+            for at in steps(k):
+                up = fe_ref[at, :]
+                parts = []
+                for s, c in enumerate(cols):
+                    e = jnp.exp2((up + c) + c_ref[at_col + s, at, :]).astype(BF16)
+                    p_ref[at, lanes(at_col + s)] = e
+                    parts.append(e.astype(F32))
+                if part:
+                    totals.append(tree(parts + [sum_ref[at, :]], add))
+                else:
+                    sum_ref[at, :] = tree(parts, add)
+            if part:
+                mine[MASS, k : k + 1, :] = jnp.sum(jnp.concatenate(totals, axis=0).T, axis=0, keepdims=True)
     post(MASS, peers_a)
 
     def wide_dot(left):
@@ -397,7 +426,10 @@
         wait_bytes(rs_a.at[g], sga.at[g])
         wait_bytes(rs_b.at[g], sgb.at[g])
     over_a = (LR1, LR2, MASS, A1, A1 + 2, A1 + 4)
-    for i in range(ROUNDS):
+    for i in range(MASS):
+        for part in range(2):
+            wait_bytes(hslots.at[i, part, pl.ds(0, len(peers_a if i in over_a else peers_b))], hsem.at[i, part])
+    for i in range(MASS, ROUNDS):
         wait_bytes(slots.at[i, pl.ds(0, len(peers_a if i in over_a else peers_b))], ssem.at[i])
     for e in range(2 * CG):
         wait_bytes(eslots.at[e, pl.ds(0, len(peers_a if e % 2 == 0 else peers_b))], essem.at[e])
@@ -453,6 +485,10 @@
             pltpu.VMEM((2, rows, ti), F32),
             pltpu.VMEM((ROUNDS, k, LANES), F32),
             pltpu.VMEM((ROUNDS, n, k, LANES), F32),
+            pltpu.VMEM((4, 2, k // 2, LANES), F32),
+            pltpu.VMEM((4, 2, n, k // 2, LANES), F32),
+            pltpu.VMEM((max(ti, tj), LANES), F32),
+            pltpu.VMEM((max(ti, tj), LANES), F32),
             pltpu.VMEM((2 * CG, 4, LANES), F32),
             pltpu.VMEM((2 * CG, n, 4, LANES), F32),
             pltpu.VMEM((2, na, half, LANES), BF16),
@@ -461,6 +497,8 @@
             pltpu.VMEM((2, nb - 1, half, LANES), BF16),
             pltpu.SemaphoreType.DMA((4,)),
             pltpu.SemaphoreType.DMA((8,)),
+            pltpu.SemaphoreType.DMA((4, 2)),
+            pltpu.SemaphoreType.DMA((4, 2)),
             pltpu.SemaphoreType.DMA((ROUNDS,)),
             pltpu.SemaphoreType.DMA((ROUNDS,)),
             pltpu.SemaphoreType.DMA((2 * CG,)),

time: 86.1 us -> 84.5 us (0.981)
  Pallas kernels: 85.3 us -> 83.7 us
    pallas_call x1, Pallas kernels: 83.9 us -> 82.3 us  [body(): pl.pallas_call(functools.partial(kernel, sizes), out_shape=(out, out), in...]
where the time goes in v5:
time: 84.5 us; the launch traced here: 84.3 us
  Pallas kernels  83.7 us (99%)
    pallas_call x1, Pallas kernels, body(): pl.pallas_call(functools.partial(kernel, sizes), out_shape=(out, out), in...  82.3 us

profile of v5, /device:TPU:1, one launch (start us, length us, event | category | flops | bytes accessed | tf_op | source)
XLA Modules:
  0.0 84.3 jit_solution(9294158937801381061)
XLA Ops:
  0.6 82.3 %transport.1 = (f32[64,64]{1,0:T(8,128)}, f32[64,64]{1,0:T(8,128)}) custom-call(bf16[64,64]{1,0:T(8,128)(2,1)} %src_hbm.1, bf16[64,64]{1,0:T(8,128)(2,1)} %tgt_hbm.1, f32[8,128]{1,0:T(8,128)} %bitcast.2, f32[8,128]{1,0:T(8,128)} %bitcast.3), custom_call_target="tpu_custom_call" | custom-call | tf_op jit(solution)/shard_map/transport/pallas_call | solution.py:455
  82.9 1.4 %hand_over.1 = (f32[64,64]{1,0:T(8,128)}, f32[64,64]{1,0:T(8,128)}) custom-call(f32[64,64]{1,0:T(8,128)} %get-tuple-element.4.one_ref, f32[64,64]{1,0:T(8,128)} %get-tuple-element.5.two_ref), custom_call_target="tpu_custom_call" | custom-call | tf_op jit(solution)/shard_map/hand_over/pallas_call | solution.py:516

commit v6 on v5

--- a/solution.py
+++ b/solution.py
@@ -28,7 +28,7 @@
     sizes, src_hbm, tgt_hbm, gf_hbm, gg_hbm, osrc_ref, otgt_ref,
     src_ref, tgt_ref, gf_ref, gg_ref,
     pack_a, pack_b, gath_a, gath_b, gown_a, gown_b, gsl_a, gsl_b,
-    x_ref, y_ref, c_ref, ct_ref, p_ref, fe_ref, lhs_ref, row_ref, xu_ref, yw_ref, xp_ref, yp_ref, yk_ref,
+    x_ref, y_ref, c_ref, ct_ref, p_ref, pt_ref, fe_ref, lhs_ref, row_ref, xu_ref, yw_ref, xp_ref, yp_ref, yk_ref,
     mine, slots, hmine, hslots, top_ref, sum_ref, emine, eslots, part_a, part_b, rs_a, rs_b,
     isem, gsem, hsem, hrsem, ssem, rsem, essem, ersem, sga, rga, sgb, rgb,
 ):
@@ -254,13 +254,15 @@
         return jnp.dot(left, p_ref[...], preferred_element_type=F32)
 
     def tall_dot(left):
-        return lax.dot_general(left, p_ref[...], (((1,), (1,)), ((), ())), preferred_element_type=F32)
+        return jnp.dot(left, pt_ref[...], preferred_element_type=F32)
 
     xp_ref[...] = wide_dot(x_ref[...])
     for s in range(kj):
         mine[CMASS, s : s + 1, :] = xp_ref[feats : feats + 1, lanes(s)]
     post(CMASS, peers_b)
-    yp_ref[...] = tall_dot(y_ref[...])
+    for k in range(ki):
+        for s in range(kj):
+            pt_ref[lanes(s), lanes(k)] = p_ref[lanes(k), lanes(s)].T
     wait_bytes(gsl_a.at[pl.ds(0, na - 1)], gsem.at[7])
     wait_bytes(gsl_b.at[pl.ds(0, nb - 1)], gsem.at[5])
     for k in range(ki):
@@ -296,6 +298,7 @@
 
     row_mass = tree(arrive(MASS, peers_a), add)
     col_dot(PULL, grad_f / row_mass)
+    yp_ref[...] = tall_dot(y_ref[...])
     col_mass = tree(arrive(CMASS, peers_b), add)
     residual = grad_g - tree(arrive(PULL, peers_b), add)
 
@@ -475,6 +478,7 @@
             pltpu.VMEM((kj, ti, LANES), F32),
             pltpu.VMEM((ki, tj, LANES), F32),
             pltpu.VMEM((ti, tj), BF16),
+            pltpu.VMEM((tj, ti), BF16),
             pltpu.VMEM((ti, LANES), F32),
             pltpu.VMEM((8, max(ti, tj)), F32),
             pltpu.VMEM((k, LANES), F32),

time: 84.5 us -> 83.7 us (level)
  Pallas kernels: 83.7 us -> 82.8 us
where the time goes in v6:
time: 83.7 us; the launch traced here: 83.5 us
  Pallas kernels  82.8 us (99%)
    pallas_call x1, Pallas kernels, body(): pl.pallas_call(functools.partial(kernel, sizes), out_shape=(out, out), in...  81.4 us

profile of v6, /device:TPU:1, one launch (start us, length us, event | category | flops | bytes accessed | tf_op | source)
XLA Modules:
  0.0 83.5 jit_solution(1282193385264809075)
XLA Ops:
  0.6 81.4 %transport.1 = (f32[64,64]{1,0:T(8,128)}, f32[64,64]{1,0:T(8,128)}) custom-call(bf16[64,64]{1,0:T(8,128)(2,1)} %src_hbm.1, bf16[64,64]{1,0:T(8,128)(2,1)} %tgt_hbm.1, f32[8,128]{1,0:T(8,128)} %bitcast.2, f32[8,128]{1,0:T(8,128)} %bitcast.3), custom_call_target="tpu_custom_call" | custom-call | tf_op jit(solution)/shard_map/transport/pallas_call | solution.py:458
  82.1 1.4 %hand_over.1 = (f32[64,64]{1,0:T(8,128)}, f32[64,64]{1,0:T(8,128)}) custom-call(f32[64,64]{1,0:T(8,128)} %get-tuple-element.4.one_ref, f32[64,64]{1,0:T(8,128)} %get-tuple-element.5.two_ref), custom_call_target="tpu_custom_call" | custom-call | tf_op jit(solution)/shard_map/hand_over/pallas_call | solution.py:520

commit v7 on v6

--- a/solution.py
+++ b/solution.py
@@ -16,8 +16,8 @@
 F32 = jnp.float32
 BF16 = jnp.bfloat16
 
-LR1, LC1, LR2, LC2, MASS, PULL, CMASS, A1 = range(8)
-ROUNDS = 12
+LR1, LC1, LR2, LC2, MASS, PULL, CMASS = range(7)
+ROUNDS = 7
 
 
 def ring(d, n):
@@ -29,8 +29,8 @@
     src_ref, tgt_ref, gf_ref, gg_ref,
     pack_a, pack_b, gath_a, gath_b, gown_a, gown_b, gsl_a, gsl_b,
     x_ref, y_ref, c_ref, ct_ref, p_ref, pt_ref, fe_ref, lhs_ref, row_ref, xu_ref, yw_ref, xp_ref, yp_ref, yk_ref,
-    mine, slots, hmine, hslots, top_ref, sum_ref, emine, eslots, part_a, part_b, rs_a, rs_b,
-    isem, gsem, hsem, hrsem, ssem, rsem, essem, ersem, sga, rga, sgb, rgb,
+    mine, slots, hmine, hslots, top_ref, sum_ref, cmine, cslots, emine, eslots, part_a, part_b, rs_a, rs_b,
+    isem, gsem, hsem, hrsem, csem, crsem, ssem, rsem, essem, ersem, sga, rga, sgb, rgb,
 ):
     nx, ny, nz, nc = sizes
     na, nb = nx * ny, nz * nc
@@ -84,6 +84,7 @@
     first1 = lax.broadcasted_iota(jnp.int32, (1, LANES), 1) < pts
     lhs_ref[...] = jnp.zeros_like(lhs_ref)
     emine[...] = jnp.zeros_like(emine)
+    cmine[...] = jnp.zeros_like(cmine)
     for ref in (x_ref, y_ref):
         pad = (ref.shape[0] - feats, ref.shape[1])
         ref[feats:, :] = (lax.broadcasted_iota(jnp.int32, pad, 0) == 0).astype(F32).astype(BF16)
@@ -288,10 +289,6 @@
         for s in range(got.shape[1] // LANES):
             mine[i, s : s + 1, :] = got[:, lanes(s)]
 
-    def row_dot(i, vector):
-        keep(i, tall_dot(load_lhs(vector, tj)))
-        post(i, peers_a)
-
     def col_dot(i, vector):
         keep(i, wide_dot(load_lhs(vector, ti)))
         post(i, peers_b)
@@ -369,21 +366,33 @@
 
         tgt_parts(1, us, ws, between)
 
+    def joint_post(r, got, peers):
+        got = got[0:1] + got[1:2] + got[2:3]
+        for s in range(got.shape[1] // LANES):
+            cmine[r, s // 4, s % 4 : s % 4 + 1, :] = got[:, lanes(s)]
+        for s, (dev, _) in enumerate(peers):
+            send(cmine.at[r], cslots.at[r, s], csem.at[r], crsem.at[r], dev)
+
+    def joint_arrive(r, peers):
+        n = len(peers)
+        wait_bytes(cslots.at[r, pl.ds(0, n)], crsem.at[r])
+        got = tree([cmine[r]] + [cslots[r, s] for s in range(n)], add)
+        groups = got.shape[0] - 1
+        return jnp.concatenate([got[t] for t in range(groups)], axis=0), jnp.sum(got[groups], axis=1, keepdims=True)
+
     dual = pulled_dual = direction = applied = norm = d_c_d = None
+    tail = cmine.shape[1] - 1
     for it in range(CG):
-        i_a, i_b = A1 + 2 * it, A1 + 2 * it + 1
-        e_a, e_b = 2 * it, 2 * it + 1
+        r_a, r_b = 2 * it, 2 * it + 1
         weighted = col_mass * residual
-        emine[e_a, 0:1, :] = line_sum(residual * residual)
-        emine[e_a, 1:2, :] = line_sum(weighted * residual)
+        cmine[r_a, tail, 0:1, :] = line_sum(residual * residual)
+        cmine[r_a, tail, 1:2, :] = line_sum(weighted * residual)
         if it:
-            emine[e_a, 2:3, :] = line_sum(weighted * direction)
-        extra_post(e_a, peers_a)
-        row_dot(i_a, residual)
+            cmine[r_a, tail, 2:3, :] = line_sum(weighted * direction)
+        joint_post(r_a, tall_dot(load_lhs(residual, tj)), peers_a)
         if it == CG - 1:
             early_gradients((grad_f - pulled_dual) / row_mass, dual, residual, direction)
-        scal = extra_arrive(e_a, peers_a)
-        fresh = tree(arrive(i_a, peers_a), add)
+        fresh, scal = joint_arrive(r_a, peers_a)
         if it:
             beta = scal[0:1] / norm
             direction = residual + beta * direction
@@ -393,19 +402,21 @@
             direction, applied, d_c_d = residual, fresh, scal[1:2]
         norm = scal[0:1]
         back = applied / row_mass
-        emine[e_b, 0:1, :] = line_sum(applied * back)
-        extra_post(e_b, peers_b)
+        q_line = line_sum(applied * back)
         if it == CG - 1:
+            emine[0, 0:1, :] = q_line
+            extra_post(0, peers_b)
             late_gradients(-back, direction, beta)
-            q_q = extra_arrive(e_b, peers_b)[0:1]
+            q_q = extra_arrive(0, peers_b)[0:1]
             alpha = norm / ((1.0 + TAU) * d_c_d - q_q)
             continue
-        col_dot(i_b, back)
-        q_q = extra_arrive(e_b, peers_b)[0:1]
-        alpha = norm / ((1.0 + TAU) * d_c_d - q_q)
+        cmine[r_b, tail, 0:1, :] = q_line
+        joint_post(r_b, wide_dot(load_lhs(back, ti)), peers_b)
+        pulled, scal = joint_arrive(r_b, peers_b)
+        alpha = norm / ((1.0 + TAU) * d_c_d - scal[0:1])
         dual = alpha * direction if it == 0 else dual + alpha * direction
         pulled_dual = alpha * applied if it == 0 else pulled_dual + alpha * applied
-        image = (1.0 + TAU) * col_mass * direction - tree(arrive(i_b, peers_b), add)
+        image = (1.0 + TAU) * col_mass * direction - pulled
         residual = residual - alpha * image
 
     def collect(g, part, me, slot, n, sem):
@@ -428,14 +439,15 @@
     for g in range(2):
         wait_bytes(rs_a.at[g], sga.at[g])
         wait_bytes(rs_b.at[g], sgb.at[g])
-    over_a = (LR1, LR2, MASS, A1, A1 + 2, A1 + 4)
+    over_a = (LR1, LR2, MASS)
     for i in range(MASS):
         for part in range(2):
             wait_bytes(hslots.at[i, part, pl.ds(0, len(peers_a if i in over_a else peers_b))], hsem.at[i, part])
     for i in range(MASS, ROUNDS):
         wait_bytes(slots.at[i, pl.ds(0, len(peers_a if i in over_a else peers_b))], ssem.at[i])
-    for e in range(2 * CG):
-        wait_bytes(eslots.at[e, pl.ds(0, len(peers_a if e % 2 == 0 else peers_b))], essem.at[e])
+    for r in range(2 * CG - 1):
+        wait_bytes(cslots.at[r, pl.ds(0, len(peers_a if r % 2 == 0 else peers_b))], csem.at[r])
+    wait_bytes(eslots.at[0, pl.ds(0, len(peers_b))], essem.at[0])
 
 
 def hand_over(one_ref, two_ref, first_ref, second_ref):
@@ -493,8 +505,10 @@
             pltpu.VMEM((4, 2, n, k // 2, LANES), F32),
             pltpu.VMEM((max(ti, tj), LANES), F32),
             pltpu.VMEM((max(ti, tj), LANES), F32),
-            pltpu.VMEM((2 * CG, 4, LANES), F32),
-            pltpu.VMEM((2 * CG, n, 4, LANES), F32),
+            pltpu.VMEM((2 * CG - 1, k // 4 + 1, 4, LANES), F32),
+            pltpu.VMEM((2 * CG - 1, n, k // 4 + 1, 4, LANES), F32),
+            pltpu.VMEM((1, 4, LANES), F32),
+            pltpu.VMEM((1, n, 4, LANES), F32),
             pltpu.VMEM((2, na, half, LANES), BF16),
             pltpu.VMEM((2, nb, half, LANES), BF16),
             pltpu.VMEM((2, na - 1, half, LANES), BF16),
@@ -503,10 +517,12 @@
             pltpu.SemaphoreType.DMA((8,)),
             pltpu.SemaphoreType.DMA((4, 2)),
             pltpu.SemaphoreType.DMA((4, 2)),
+            pltpu.SemaphoreType.DMA((2 * CG - 1,)),
+            pltpu.SemaphoreType.DMA((2 * CG - 1,)),
             pltpu.SemaphoreType.DMA((ROUNDS,)),
             pltpu.SemaphoreType.DMA((ROUNDS,)),
-            pltpu.SemaphoreType.DMA((2 * CG,)),
-            pltpu.SemaphoreType.DMA((2 * CG,)),
+            pltpu.SemaphoreType.DMA((1,)),
+            pltpu.SemaphoreType.DMA((1,)),
             pltpu.SemaphoreType.DMA((2,)),
             pltpu.SemaphoreType.DMA((2,)),
             pltpu.SemaphoreType.DMA((2,)),

time: 83.7 us -> 83.5 us (level)
  no operation moved by 1% of the time
where the time goes in v7:
time: 83.5 us; the launch traced here: 83.2 us
  Pallas kernels  82.6 us (99%)
    pallas_call x1, Pallas kernels, body(): pl.pallas_call(functools.partial(kernel, sizes), out_shape=(out, out), in...  81.2 us

profile of v7, /device:TPU:1, one launch (start us, length us, event | category | flops | bytes accessed | tf_op | source)
XLA Modules:
  0.0 83.2 jit_solution(12974173135464407262)
XLA Ops:
  0.6 81.2 %transport.1 = (f32[64,64]{1,0:T(8,128)}, f32[64,64]{1,0:T(8,128)}) custom-call(bf16[64,64]{1,0:T(8,128)(2,1)} %src_hbm.1, bf16[64,64]{1,0:T(8,128)(2,1)} %tgt_hbm.1, f32[8,128]{1,0:T(8,128)} %bitcast.2, f32[8,128]{1,0:T(8,128)} %bitcast.3), custom_call_target="tpu_custom_call" | custom-call | tf_op jit(solution)/shard_map/transport/pallas_call | solution.py:470
  81.8 1.4 %hand_over.1 = (f32[64,64]{1,0:T(8,128)}, f32[64,64]{1,0:T(8,128)}) custom-call(f32[64,64]{1,0:T(8,128)} %get-tuple-element.4.one_ref, f32[64,64]{1,0:T(8,128)} %get-tuple-element.5.two_ref), custom_call_target="tpu_custom_call" | custom-call | tf_op jit(solution)/shard_map/hand_over/pallas_call | solution.py:536
